TPU v7x, 128 devices: a whole 4x4x4 slice. The times are simulated.
128 devices in a mesh: chan: 16 (over y_lo, z, core), feed: 8 (over x, y_hi).
Axes of the slice: x: 4, y: 4 (y_hi: 2, y_lo: 2; y = y_hi * 2 + y_lo), z: 4, core: 2. Of those that a mesh axis runs over, the one named last changes fastest.
Arguments:
- raw_volts: bfloat16 [2048, 268288], P(('chan', 'feed')), may hold values from -6 to 6
- channel_gains: float32 [2, 64, 2048], P(None, None, ('chan', 'feed')), may hold values from -7 to 7
- feed_flags: int32 [2048], replicated, may hold values 0 or 1
- steer_index: int32 [512, 2048], P(None, 'feed'), may hold values from 0 to 255
Outputs:
- visibility: float32 [2, 64, 2048, 2048], P(None, 'chan', 'feed')
- beam_power: float32 [512, 64, 128], P('feed', 'chan')
All inputs are finite; a program needn't handle non-finite values.
Results may differ from a plain program's by a relative error of at most 0.0053.
Values may be sent and summed in bfloat16 or wider, within the bound.
A program may use at most 128 MiB of HBM per device.

v0:
```python
import jax
import jax.numpy as jnp
from jax import lax
from jax.sharding import PartitionSpec as P

CHANS = 1024
TAPS = 4
PHASES = 256


EPSILON = 1e-06


def filter_table(band_count):
    block_len = 2 * CHANS
    full_len = TAPS * block_len
    band_first = CHANS // 2 - band_count // 2
    sample_pos = jnp.arange(full_len, dtype=jnp.float32)
    centred = (sample_pos + 0.5) / full_len - 0.5
    window = jnp.sinc(TAPS * centred) * (
        0.5 - 0.5 * jnp.cos(2.0 * jnp.pi * (sample_pos + 0.5) / full_len)
    )
    window = window / jnp.sqrt(jnp.sum(window * window))
    within = jnp.arange(block_len, dtype=jnp.int32)
    channel = band_first + jnp.arange(band_count, dtype=jnp.int32)
    turn_count = within[:, None] * channel[None, :] % block_len
    phase_angle = 2.0 * jnp.pi / block_len * turn_count.astype(jnp.float32)
    weights = window.reshape(TAPS, block_len)[:, :, None]
    combined = jnp.concatenate(
        [weights * jnp.cos(phase_angle)[None], -(weights * jnp.sin(phase_angle)[None])], axis=2
    )
    return combined.astype(jnp.bfloat16)


def channelize(volt_rows, table):
    row_count = volt_rows.shape[0]
    block_len = 2 * CHANS
    spectra = volt_rows.shape[1] // block_len - TAPS + 1
    blocks = volt_rows.reshape(row_count, spectra + TAPS - 1, block_len)
    summed = jnp.zeros((row_count * spectra, table.shape[2]), jnp.float32)
    for tap_index in range(TAPS):
        frames = blocks[:, tap_index : tap_index + spectra].reshape(row_count * spectra, block_len)
        summed = summed + jnp.dot(frames, table[tap_index], preferred_element_type=jnp.float32)
    return summed.reshape(row_count, spectra, table.shape[2])


def apply_gains(raw_spectra, gain_rows):
    band_count = raw_spectra.shape[2] // 2
    real_part = raw_spectra[:, :, :band_count]
    imag_part = raw_spectra[:, :, band_count:]
    gain_re = gain_rows[0].T[:, None, :]
    gain_im = gain_rows[1].T[:, None, :]
    real_spec = (gain_re * real_part - gain_im * imag_part).astype(jnp.bfloat16)
    imag_spec = (gain_re * imag_part + gain_im * real_part).astype(jnp.bfloat16)
    return (real_spec, imag_spec)


def squared_sum(spectra_block):
    wide = spectra_block.astype(jnp.float32)
    return jnp.sum(wide * wide, axis=(0, 1, 2))


def on_device(raw_volts, channel_gains, feed_flags, steer_index):
    chan_count = lax.axis_size("chan")
    feed_count = lax.axis_size("feed")
    band_count = channel_gains.shape[1]
    table = filter_table(band_count)
    raw_spectra = channelize(raw_volts, table)
    real_spec, imag_spec = apply_gains(raw_spectra, channel_gains)
    local_spectra = jnp.transpose(jnp.stack([real_spec, imag_spec], axis=0), (3, 0, 2, 1))
    own_inputs = local_spectra.shape[3]
    spectra = local_spectra.shape[2]
    per_chan = band_count // chan_count
    sorted_chan = lax.all_to_all(local_spectra, "chan", split_axis=0, concat_axis=3, tiled=True)
    grouped = lax.all_gather(sorted_chan, "feed", axis=3, tiled=True)
    grouped = grouped.reshape(per_chan, 2, spectra, feed_count, chan_count, own_inputs)
    turned = jnp.transpose(grouped, (0, 1, 2, 4, 3, 5)).reshape(
        per_chan, 2, spectra, chan_count * feed_count * own_inputs
    )
    band_total = lax.psum(squared_sum(turned), "chan")
    band_mean = band_total / (band_count * spectra)
    inverse_rms = lax.rsqrt(band_mean + EPSILON)
    all_inputs = turned.shape[3]
    group_size = all_inputs // feed_count
    first_input = lax.axis_index("feed") * group_size
    masked = turned * feed_flags.astype(jnp.bfloat16)
    own_rows = lax.dynamic_slice_in_dim(masked, first_input, group_size, 3)
    swapped = jnp.stack([own_rows[:, 1], -own_rows[:, 0]], axis=1)
    contract = (((1, 2), (1, 2)), ((0,), (0,)))
    real_vis = lax.dot_general(own_rows, masked, contract, preferred_element_type=jnp.float32)
    imag_vis = lax.dot_general(swapped, masked, contract, preferred_element_type=jnp.float32)
    own_scale = lax.dynamic_slice_in_dim(inverse_rms, first_input, group_size, 0)
    pair_weight = (own_scale[:, None] * inverse_rms[None, :] / spectra)[None]
    visibility = jnp.stack([real_vis * pair_weight, imag_vis * pair_weight], axis=0)
    own_re = own_rows[:, 0]
    own_im = own_rows[:, 1]
    phase_angle = 2.0 * jnp.pi / PHASES * steer_index.astype(jnp.float32)
    cos_weight = jnp.cos(phase_angle).astype(jnp.bfloat16)
    sin_weight = jnp.sin(phase_angle).astype(jnp.bfloat16)
    beam_re = jnp.einsum(
        "bg,ctg->bct", cos_weight, own_re, preferred_element_type=jnp.float32
    ) - jnp.einsum("bg,ctg->bct", sin_weight, own_im, preferred_element_type=jnp.float32)
    beam_im = jnp.einsum(
        "bg,ctg->bct", sin_weight, own_re, preferred_element_type=jnp.float32
    ) + jnp.einsum("bg,ctg->bct", cos_weight, own_im, preferred_element_type=jnp.float32)
    beam_local = lax.psum_scatter(
        jnp.stack([beam_re, beam_im], axis=1), "feed", scatter_dimension=0, tiled=True
    )
    beam_power = (
        beam_local[:, 0] * beam_local[:, 0] + beam_local[:, 1] * beam_local[:, 1]
    ) / all_inputs
    return (visibility, beam_power)


def solution(mesh):
    in_specs = (P(("chan", "feed"), None), P(None, None, ("chan", "feed")), P(), P(None, "feed"))
    out_specs = (P(None, "chan", "feed", None), P("feed", "chan", None))
    return jax.shard_map(
        on_device, mesh=mesh, in_specs=in_specs, out_specs=out_specs, check_vma=False
    )
```

profile of v0, /device:TPU:0, one launch (start us, length us, event | category | flops | bytes accessed | tf_op | source)
XLA Modules:
  0.0 248.8 jit_solution(10904308962179305782)
XLA Ops:
  7.2 0.8 fusion.70
  8.0 12.7 %reshape.172 = bf16[16,131,2048]{2,1,0:T(8,128)(2,1)} reshape(bf16[16,268288]{1,0:T(8,128)(2,1)} %param.4) | data formatting | bytes 17170432 | tf_op jit(solution)/shard_map/reshape | solution.py:39
  20.7 24.3 %fusion.88 = (bf16[16,128,2048]{2,1,0:T(8,128)(2,1)}, bf16[16,128,2048]{2,1,0:T(8,128)(2,1)}, bf16[16,128,2048]{2,1,0:T(8,128)(2,1)}, bf16[16,128,2048]{2,1,0:T(8,128)(2,1)}) fusion(bf16[16,131,2048]{2,1,0:T(8,128)(2,1)} %reshape.172), kind=kLoop, calls=%fused_computation.141 | loop fusion | bytes 67108864 | tf_op jit(solution)/shard_map/slice | solution.py:42
  45.0 2.1 fusion.38
  47.8 0.3 fusion.64
  48.1 0.4 negate_convert_fusion
  48.5 6.4 %fusion.13 = f32[128,2048]{1,0:T(8,128)S(1)} fusion(bf16[2048,2048]{1,0:T(8,128)(2,1)} %bitcast.98, bf16[4,2048,64]{1,2,0:T(8,128)(2,1)S(1)} %get-tuple-element.23, bf16[4,2048,64]{1,2,0:T(8,128)(2,1)S(1)} %get-tuple-element.22), kind=kOutput, calls=%fused_computation.35 | convolution fusion | flops 1074790400 | bytes 11534336 | tf_op jit(solution)/shard_map/dot_general | solution.py:43
  55.0 2.9 %convolution_add_fusion.2 = f32[128,2048]{1,0:T(8,128)S(1)} fusion(f32[128,2048]{1,0:T(8,128)S(1)} %fusion.13, bf16[2048,2048]{1,0:T(8,128)(2,1)S(1)} %bitcast.97, bf16[4,2048,64]{1,2,0:T(8,128)(2,1)S(1)} %get-tuple-element.23, bf16[4,2048,64]{1,2,0:T(8,128)(2,1)S(1)} %get-tuple-element.22), kind=kOutput, calls=%fused_computation.15 | convolution fusion | flops 1075052544 | bytes 12582912 | tf_op jit(solution)/shard_map/dot_general | solution.py:43
  57.9 2.9 %convolution_add_fusion.1 = f32[128,2048]{1,0:T(8,128)S(1)} fusion(f32[128,2048]{1,0:T(8,128)S(1)} %convolution_add_fusion.2, bf16[2048,2048]{1,0:T(8,128)(2,1)S(1)} %bitcast.96, bf16[4,2048,64]{1,2,0:T(8,128)(2,1)S(1)} %get-tuple-element.23, bf16[4,2048,64]{1,2,0:T(8,128)(2,1)S(1)} %get-tuple-element.22), kind=kOutput, calls=%fused_computation.14 | convolution fusion | flops 1075052544 | bytes 12582912 | tf_op jit(solution)/shard_map/dot_general | solution.py:43
  60.8 2.9 %fusion.2 = f32[16,8,16,128]{3,1,2,0:T(8,128)S(1)} fusion(f32[128,2048]{1,0:T(8,128)S(1)} %convolution_add_fusion.1, bf16[2048,2048]{1,0:T(8,128)(2,1)S(1)} %bitcast.93, bf16[4,2048,64]{1,2,0:T(8,128)(2,1)S(1)} %get-tuple-element.22, bf16[4,2048,64]{1,2,0:T(8,128)(2,1)S(1)} %get-tuple-element.23), kind=kOutput, calls=%fused_computation.20 | convolution fusion | flops 1075052544 | bytes 12582912 | tf_op jit(solution)/shard_map/dot_general | solution.py:43
  63.7 0.2 copy.83
  64.1 0.3 fusion.28
  64.5 17.2 %all_to_all.18 = bf16[64,2,128,16]{2,3,1,0:T(8,128)(2,1)S(1)} all-to-all(bf16[64,2,128,16]{2,3,1,0:T(8,128)(2,1)S(1)} %maximum_bitcast_fusion), channel_id=1, replica_groups=mesh['chan'=16,'feed'=8] {'chan'}, dimensions={0} | all-to-all | bytes 1048576 | tf_op jit(solution)/shard_map/all_to_all | solution.py:74
  81.7 0.8 copy.65
  82.5 0.3 reduce-scatter.2.cloned.1.call-start
  82.8 70.3 %all-gather.2.cloned.1.call-done = bf16[4,2,128,2048]{2,3,1,0:T(8,128)(2,1)} async-done(((bf16[4,2,128,256]{2,3,1,0:T(8,128)(2,1)}), bf16[4,2,128,2048]{2,3,1,0:T(8,128)(2,1)}) %all-gather.2.cloned.1.call-update) | async-done | bytes 4194320 | tf_op jit(solution)/shard_map/all_gather | solution.py:75
  153.2 3.4 %copy.66 = bf16[4,2,128,16,8,16]{2,5,4,3,1,0:T(8,128)(2,1)S(1)} copy(bf16[4,2,128,16,8,16]{2,5,3,4,1,0:T(8,128)(2,1)} %bitcast.99) | data formatting | bytes 8388608 | tf_op jit(solution)/shard_map/transpose | solution.py:77
  156.6 1.0 bitcast_multiply_fusion.2
  157.6 1.8 fusion.34
  159.5 1.8 fusion.36
  161.4 1.9 fusion.3
  163.3 1.9 fusion.4
  165.2 1.5 pad_maximum_fusion.1
  166.7 3.1 %multiply_reduce_fusion = f32[16,8,16]{2,0,1:T(8,128)S(1)} fusion(bf16[4,2,128,16,8,16]{2,5,3,4,1,0:T(8,128)(2,1)} %bitcast.100), kind=kLoop, calls=%fused_computation.5 | loop fusion | flops 6289408 | bytes 4202496 | tf_op jit(solution)/shard_map/reduce_sum | solution.py:60
  169.9 29.9 %psum.7 = f32[2048]{0:T(1024)S(1)} all-reduce(f32[2048]{0:T(1024)S(1)} %reduce_sum.22), channel_id=1, replica_groups=mesh['chan'=16,'feed'=8] {'chan'}, use_global_device_ids=true, to_apply=%region_2.3 | all-reduce | flops 2048 | bytes 16384 | tf_op jit(solution)/shard_map/psum | solution.py:80
  199.9 0.2 multiply_multiply_fusion
  200.1 4.0 %fusion.1 = f32[1,4,256,2048]{3,2,1,0:T(8,128)S(1)} fusion(bf16[4,2,128,2048]{2,3,1,0:T(8,128)(2,1)} %copy-done, f32[256,2048]{1,0:T(8,128)S(1)} %multiply_multiply_fusion, s32[]{:T(128)S(6)} %select_n.83), kind=kOutput, calls=%fused_computation.4 | convolution fusion | flops 1075838976 | bytes 15204356 | tf_op jit(solution)/shard_map/dot_general | solution.py:90
  204.1 1.3 fusion
  205.4 6.4 %pad_maximum_fusion = f32[2,4,256,2048]{3,2,1,0:T(8,128)} fusion(f32[1,4,256,2048]{3,2,1,0:T(8,128)S(1)} %fusion, f32[1,4,256,2048]{3,2,1,0:T(8,128)S(1)} %fusion.1), kind=kLoop, calls=%fused_computation | loop fusion | flops 4194304 | bytes 33554432 | tf_op jit(solution)/shard_map/stack | solution.py:94
  211.9 28.3 %reduce-scatter.2.cloned.1.call-done = f32[64,2,4,128]{3,0,2,1:T(8,128)} async-done(((f32[512,2,4,128]{3,0,2,1:T(8,128)}), f32[64,2,4,128]{3,0,2,1:T(8,128)}) %reduce-scatter.2.cloned.1.call-update) | async-done | bytes 262160 | tf_op jit(solution)/shard_map/reduce_scatter | solution.py:106
  240.2 1.0 fusion.44
  241.2 0.7 copy.74
  (36 shorter events, 0.7 us)
Async XLA Ops:
  7.2 146.0 %all-gather.2.cloned.1.call-start = ((), (), s32[]{:S(2)}) async-start(), calls=%async_computation.2 | async-start | bytes 4718592 | tf_op jit(solution)/shard_map/all_gather | solution.py:75
  48.1 6.8 %copy-start.2 = (bf16[16,128,2048]{2,1,0:T(8,128)(2,1)S(1)}, bf16[16,128,2048]{2,1,0:T(8,128)(2,1)}, u32[]{:S(2)}) copy-start(bf16[16,128,2048]{2,1,0:T(8,128)(2,1)} %get-tuple-element.16) | copy-start | bytes 25165828
  48.5 9.4 %slice-start.2 = ((s8[8388608]{0:T(1024)(128)(4,1)}), s8[4194304]{0:T(1024)(128)(4,1)S(1)}, s32[]{:S(2)}) async-start(s8[8388608]{0:T(1024)(128)(4,1)} %bitcast.94), calls=%async_computation.6 | async-start | bytes 8388608
  55.0 2.9 %slice-start.3 = ((s8[8388608]{0:T(1024)(128)(4,1)}), s8[4194304]{0:T(1024)(128)(4,1)S(1)}, s32[]{:S(2)}) async-start(s8[8388608]{0:T(1024)(128)(4,1)} %bitcast.94), calls=%async_computation.7 | async-start | bytes 8388608
  55.0 5.8 %slice-start = ((s8[8388608]{0:T(1024)(128)(4,1)}), s8[4194304]{0:T(1024)(128)(4,1)S(1)}, s32[]{:S(2)}) async-start(s8[8388608]{0:T(1024)(128)(4,1)} %bitcast.91), calls=%async_computation.4 | async-start | bytes 8388608
  57.9 2.9 %slice-start.1 = ((s8[8388608]{0:T(1024)(128)(4,1)}), s8[4194304]{0:T(1024)(128)(4,1)S(1)}, s32[]{:S(2)}) async-start(s8[8388608]{0:T(1024)(128)(4,1)} %bitcast.91), calls=%async_computation.5 | async-start | bytes 8388608
  60.8 3.1 %copy-start.4 = (f32[2,64,16]{1,2,0:T(8,128)S(1)}, f32[2,64,16]{1,2,0:T(8,128)}, u32[]{:S(2)}) copy-start(f32[2,64,16]{1,2,0:T(8,128)} %param.5) | copy-start | bytes 24580
  63.7 19.1 %copy-start.5 = (s32[2048]{0:T(1024)S(1)}, s32[2048]{0:T(1024)}, u32[]{:S(2)}) copy-start(s32[2048]{0:T(1024)} %param.6) | copy-start | bytes 24580
  82.5 157.7 %reduce-scatter.2.cloned.1.call-start = ((), (), s32[]{:S(2)}) async-start(), calls=%async_computation.3 | async-start | bytes 2359296 | tf_op jit(solution)/shard_map/reduce_scatter | solution.py:106
  156.6 1.0 copy-start.3
  157.6 7.6 %copy-start = (bf16[4,2,128,2048]{2,3,1,0:T(8,128)(2,1)}, bf16[4,2,128,2048]{2,3,1,0:T(8,128)(2,1)S(1)}, u32[]{:S(2)}) copy-start(bf16[4,2,128,2048]{2,3,1,0:T(8,128)(2,1)S(1)} %bitcast_multiply_fusion.2) | copy-start | bytes 12582916
  200.1 4.0 %copy-start.1 = (bf16[4,2,128,2048]{2,3,1,0:T(8,128)(2,1)S(1)}, bf16[4,2,128,2048]{2,3,1,0:T(8,128)(2,1)}, u32[]{:S(2)}) copy-start(bf16[4,2,128,2048]{2,3,1,0:T(8,128)(2,1)} %copy-done) | copy-start | bytes 12582916
Sparse Core Ops, SparseCore 0:
  82.6 70.4 all-gather.1
  166.8 73.3 reduce-scatter.1
where the time goes:
time: 249 us
  waiting for transfers between devices  98.7 us (40%)
  blocking collectives  47.1 us (19%)
  local copies, waits for them, and re-layouts  42.6 us (17%)
  matrix products  27.8 us (11%)
  other arithmetic  17.2 us (7%)
  between operations  15.1 us (6%)
    all_gather x1, waiting for transfers between devices, on_device(): grouped = lax.all_gather(sorted_chan, 'feed', axis=3, tiled=True)  70.3 us
    psum x1, blocking collectives, on_device(): band_total = lax.psum(squared_sum(turned), 'chan')  29.9 us
    reduce_scatter x1, waiting for transfers between devices, on_device(): lax.psum_scatter(jnp.stack([beam_re, beam_im], axis=1), 'feed', scatter_d...  28.3 us
    slice x1, local copies, waits for them, and re-layouts, channelize(): blocks[:, tap_index:tap_index + spectra]  24.3 us
    all_to_all x1, blocking collectives, on_device(): lax.all_to_all(local_spectra, 'chan', split_axis=0, concat_axis=3, tiled=...  17.2 us
    dot_general x4, matrix products, channelize(): jnp.dot(frames, table[tap_index], preferred_element_type=jnp.float32)  15 us
    reshape x1, local copies, waits for them, and re-layouts, channelize(): blocks = volt_rows.reshape(row_count, spectra + TAPS - 1, block_len)  12.7 us
    another operation x1, other arithmetic, on_device(): jnp.stack([real_vis * pair_weight, imag_vis * pair_weight], axis=0)  6.44 us
  transfers between devices with their start and end apart: 2, of which 2 were waited for; matrix products, arithmetic and copies ran while one was open for 6% of the time, Pallas kernels for 0%

commit v1 on v0

v1 whole, which is shorter than its diff:
```python
import functools

import jax
import jax.numpy as jnp
import ml_dtypes
import numpy as np
from jax import lax
from jax.experimental import pallas as pl
from jax.experimental.pallas import tpu as pltpu
from jax.sharding import PartitionSpec as P

CHANS = 1024
INPUTS = 2048
TAPS = 4
PHASES = 256
NT = 128
BAND = 64
BEAMS = 512
BLOCK = 2 * CHANS
EPSILON = 1e-06

CHAN_DEVS = 16
FEED_DEVS = 8
OWN = 16
PER_CHAN = BAND // CHAN_DEVS
UNIT = PER_CHAN * OWN
HALF_T = NT // 2
SLABS = NT + TAPS - 1
SUBS = 2
SUB = CHAN_DEVS // SUBS
OWN_BEAMS = BEAMS // FEED_DEVS
FEED_INPUTS = INPUTS // FEED_DEVS
KINDS = 7
FIRST_SLABS = 68
MESH = pl.DeviceIdType.MESH


def filter_table():
    full_len = TAPS * BLOCK
    pos = np.arange(full_len, dtype=np.float64)
    centred = (pos + 0.5) / full_len - 0.5
    window = np.sinc(TAPS * centred) * (0.5 - 0.5 * np.cos(2.0 * np.pi * (pos + 0.5) / full_len))
    window = window / np.sqrt(np.sum(window * window))
    channel = CHANS // 2 - BAND // 2 + np.arange(BAND)
    turn = (np.arange(BLOCK)[:, None] * channel[None, :]) % BLOCK
    angle = 2.0 * np.pi / BLOCK * turn
    weights = window.reshape(TAPS, BLOCK)[:, :, None]
    table = np.concatenate([weights * np.cos(angle), -(weights * np.sin(angle))], axis=2)
    return np.transpose(table, (1, 0, 2)).reshape(BLOCK, TAPS * 2 * BAND).astype(ml_dtypes.bfloat16)


def turn_kernel(
    raw, table, gains, steer, flags, spectra, powers, weights,
    volts, tab, conv, summed, turned, outbox, gain_sq, power_acc, power_row,
    steer_out, steer_in, weight_buf,
    load_sem, tab_sem, own_sem, a_send, a_recv, b_send, b_recv,
    s_send, s_recv, p_send, p_recv, q_send, q_recv, out_sem,
):
    chan = lax.axis_index("chan")
    feed = lax.axis_index("feed")
    x = feed // 2
    row = feed % 2

    def feed_at(dx, across):
        r = 1 - row if across else row
        return lax.rem(x + dx + 4, 4) * 2 + r

    right = (chan, feed_at(1, False))
    left = (chan, feed_at(-1, False))
    over = (chan, feed_at(0, True))

    barrier = pltpu.get_barrier_semaphore()
    for d in range(1, CHAN_DEVS):
        pl.semaphore_signal(
            barrier, inc=1, device_id=(lax.rem(chan + d, CHAN_DEVS), feed), device_id_type=MESH
        )
    for d in range(1, FEED_DEVS):
        pl.semaphore_signal(
            barrier, inc=1, device_id=(chan, lax.rem(feed + d, FEED_DEVS)), device_id_type=MESH
        )

    tab_copy = pltpu.make_async_copy(table, tab, tab_sem)
    tab_copy.start()
    groups = [(0, 34), (34, 34), (68, 32), (100, 31)]
    for g, (first, count) in enumerate(groups):

        @pl.loop(0, count)
        def _(n):
            s = first + n
            pltpu.make_async_copy(
                raw.at[:, pl.ds(pl.multiple_of(s * BLOCK, BLOCK), BLOCK)],
                volts.at[pl.ds(pl.multiple_of(s * OWN, OWN), OWN), :],
                load_sem.at[g],
            ).start()

    steer_out[...] = steer[...].astype(jnp.float32).astype(jnp.bfloat16)

    gain_sq[...] = jnp.zeros_like(gain_sq)
    gain_sq[0:BAND, 0:OWN] = gains[0]
    gain_sq[BAND : 2 * BAND, 0:OWN] = gains[1]
    gain_rows = gain_sq[...].T[0:OWN]
    lane8 = lax.broadcasted_iota(jnp.int32, (8, 128), 1)
    low8 = lane8 < BAND
    g_lo, g_hi = gain_rows[0:8], gain_rows[8:16]
    pair_re = jnp.where(low8, g_lo, pltpu.roll(g_hi, BAND, 1))
    pair_im = jnp.where(low8, pltpu.roll(g_lo, BAND, 1), g_hi)

    pl.semaphore_wait(barrier, CHAN_DEVS + FEED_DEVS - 2)

    steer_copies = []
    for d in range(1, FEED_DEVS):
        other = lax.rem(feed + d, FEED_DEVS)
        steer_copies.append(
            pltpu.make_async_remote_copy(
                src_ref=steer_out.at[pl.ds(pl.multiple_of(other * OWN_BEAMS, OWN_BEAMS), OWN_BEAMS), :],
                dst_ref=steer_in.at[feed],
                send_sem=s_send.at[d],
                recv_sem=s_recv.at[d],
                device_id=(chan, other),
                device_id_type=MESH,
            )
        )
        steer_copies[-1].start()
    own_steer = pltpu.make_async_copy(
        steer_out.at[pl.ds(pl.multiple_of(feed * OWN_BEAMS, OWN_BEAMS), OWN_BEAMS), :],
        steer_in.at[feed],
        s_send.at[0],
    )
    own_steer.start()

    low = lax.broadcasted_iota(jnp.int32, (HALF_T, 128), 1) < BAND

    def loaded(g):
        first, count = groups[g]
        rows = volts.at[pl.ds(first * OWN, count * OWN), :]
        pltpu.make_async_copy(rows, rows, load_sem.at[g]).wait()

    def convolve(first, count):
        conv[pl.ds(first * OWN, count * OWN), :] = jnp.dot(
            volts[pl.ds(first * OWN, count * OWN), :], tab[...], preferred_element_type=jnp.float32
        )

    def turn(h):
        total = None
        for k in range(TAPS):
            part = conv[pl.ds((HALF_T * h + k) * OWN, HALF_T * OWN), 128 * k : 128 * (k + 1)]
            total = part if total is None else total + part
        summed[...] = total
        for i in range(8):
            a = summed[pl.ds(i, HALF_T, stride=OWN), :]
            b = summed[pl.ds(i + 8, HALF_T, stride=OWN), :]
            re = jnp.where(low, a, pltpu.roll(b, BAND, 1))
            im = jnp.where(low, pltpu.roll(a, BAND, 1), b)
            g_re = pair_re[i : i + 1]
            g_im = pair_im[i : i + 1]
            spec_re = (g_re * re - g_im * im).astype(jnp.bfloat16).astype(jnp.float32)
            spec_im = (g_re * im + g_im * re).astype(jnp.bfloat16).astype(jnp.float32)
            power = spec_re * spec_re + spec_im * spec_im
            power = jnp.sum(power.reshape(HALF_T // 8, 8, 128), axis=0)
            if h == 0:
                power_acc[i] = power
            else:
                power_acc[i] = power_acc[i] + power
            flipped = jnp.concatenate([spec_re, spec_im], axis=0).T
            turned[pl.ds(i, BAND, stride=OWN), :] = flipped[0:BAND]
            turned[pl.ds(i + 8, BAND, stride=OWN), :] = flipped[BAND : 2 * BAND]
        outbox[h] = turned[...].astype(jnp.bfloat16)

    a_copies = []

    def send_chan(h):
        mine = pltpu.make_async_copy(
            outbox.at[h, pl.ds(pl.multiple_of(chan * UNIT, UNIT), UNIT), :],
            spectra.at[h, chan, feed],
            own_sem.at[h],
        )
        mine.start()
        for d in range(1, CHAN_DEVS):
            other = lax.rem(chan + d, CHAN_DEVS)
            copy = pltpu.make_async_remote_copy(
                src_ref=outbox.at[h, pl.ds(pl.multiple_of(other * UNIT, UNIT), UNIT), :],
                dst_ref=spectra.at[h, chan, feed],
                send_sem=a_send.at[h, d],
                recv_sem=a_recv.at[h, chan // SUB],
                device_id=(other, feed),
                device_id_type=MESH,
            )
            copy.start()
            a_copies.append(copy)
        return mine

    def arrived(h, sub, count):
        rows = spectra.at[h, pl.ds(0, count), 0]
        pltpu.make_async_copy(rows, rows, a_recv.at[h, sub]).wait()

    sub_of = [chan // SUB, 1 - chan // SUB]

    def spread(h, n, kind, origin, target):
        block = spectra.at[h, pl.ds(pl.multiple_of(sub_of[n] * SUB, SUB), SUB), origin]
        return pltpu.make_async_remote_copy(
            src_ref=block,
            dst_ref=block,
            send_sem=b_send.at[h, kind, n],
            recv_sem=b_recv.at[h, kind, n],
            device_id=target,
            device_id_type=MESH,
        )

    plans = []
    for h in range(2):
        fore, back = (right, left) if h == 0 else (left, right)
        s = 1 if h == 0 else -1
        plans.append(
            [
                (feed, fore),
                (feed, back),
                (feed, over),
                (feed_at(-s, False), fore),
                (feed_at(s, False), over),
                (feed_at(0, True), fore),
                (feed_at(s, True), back),
            ]
        )
    made = {}

    def start(h, n, kind):
        origin, target = plans[h][kind]
        made[h, n, kind] = spread(h, n, kind, origin, target)
        made[h, n, kind].start()

    def landed(h, n, kind):
        made[h, n, kind].wait_recv()

    def step_one(h, n, mine):
        if n == 0:
            mine.wait()
            arrived(h, sub_of[0], SUB - 1)
        else:
            arrived(h, sub_of[1], SUB)
        for kind in (2, 0, 1):
            start(h, n, kind)

    loaded(0)
    tab_copy.wait()
    convolve(0, 34)
    loaded(1)
    convolve(34, 34)
    turn(0)
    mine0 = send_chan(0)
    loaded(2)
    convolve(67, 33)
    loaded(3)
    convolve(100, 31)
    step_one(0, 0, mine0)
    turn(1)
    mine1 = send_chan(1)
    step_one(0, 1, mine0)

    sums = jnp.sum(power_acc[...], axis=1)
    first = jnp.sum(jnp.where(low8, sums, 0.0), axis=1, keepdims=True)
    second = jnp.sum(jnp.where(low8, 0.0, sums), axis=1, keepdims=True)
    column = jnp.concatenate([first, second], axis=0)
    lane16 = lax.broadcasted_iota(jnp.int32, (OWN, 128), 1)
    sub16 = lax.broadcasted_iota(jnp.int32, (OWN, 128), 0)
    power_row[...] = jnp.sum(
        jnp.where(lax.rem(lane16, OWN) == sub16, column, 0.0), axis=0, keepdims=True
    )
    p_own = pltpu.make_async_copy(power_row, powers.at[feed, chan], own_sem.at[2])
    p_own.start()
    p_copies = []
    for d in range(1, CHAN_DEVS):
        copy = pltpu.make_async_remote_copy(
            src_ref=power_row,
            dst_ref=powers.at[feed, chan],
            send_sem=p_send.at[d],
            recv_sem=p_recv.at[d],
            device_id=(lax.rem(chan + d, CHAN_DEVS), feed),
            device_id_type=MESH,
        )
        copy.start()
        p_copies.append(copy)

    step_one(1, 0, mine1)
    step_one(1, 1, mine1)

    for copy in steer_copies:
        copy.wait()
    own_steer.wait()
    for g in range(FEED_DEVS):
        cols = pl.ds(g * FEED_INPUTS, FEED_INPUTS)
        index = steer_in[g].astype(jnp.float32)
        quarter = jnp.floor((index + 32.0) * (1.0 / 64.0))
        angle = (index - 64.0 * quarter) * (2.0 * np.pi / PHASES)
        sq = angle * angle
        cos = 1.0 + sq * (-1.0 / 2 + sq * (1.0 / 24 + sq * (-1.0 / 720 + sq * (1.0 / 40320))))
        sin = angle * (
            1.0 + sq * (-1.0 / 6 + sq * (1.0 / 120 + sq * (-1.0 / 5040 + sq * (1.0 / 362880))))
        )
        swap = (quarter == 1.0) | (quarter == 3.0)
        cos_neg = (quarter == 1.0) | (quarter == 2.0)
        sin_neg = (quarter == 2.0) | (quarter == 3.0)
        cos_mag = jnp.where(swap, sin, cos)
        sin_mag = jnp.where(swap, cos, sin)
        good = flags[:, cols].astype(jnp.float32)
        weight_buf[0:OWN_BEAMS, cols] = (jnp.where(cos_neg, -cos_mag, cos_mag) * good).astype(
            jnp.bfloat16
        )
        weight_buf[OWN_BEAMS : 2 * OWN_BEAMS, cols] = (
            jnp.where(sin_neg, -sin_mag, sin_mag) * good
        ).astype(jnp.bfloat16)
    weight_copy = pltpu.make_async_copy(weight_buf, weights, out_sem)
    weight_copy.start()

    for h in range(2):
        fore_in, back_in = 0, 1
        for n in range(SUBS):
            landed(h, n, back_in)
            start(h, n, 4)
            landed(h, n, fore_in)
            start(h, n, 3)
            landed(h, n, 2)
            start(h, n, 5)

    p_own.wait()
    for copy in p_copies:
        copy.wait()
    q_copies = []
    for d in range(1, FEED_DEVS):
        copy = pltpu.make_async_remote_copy(
            src_ref=powers.at[feed],
            dst_ref=powers.at[feed],
            send_sem=q_send.at[d],
            recv_sem=q_recv.at[d],
            device_id=(chan, lax.rem(feed + d, FEED_DEVS)),
            device_id_type=MESH,
        )
        copy.start()
        q_copies.append(copy)

    for h in range(2):
        for n in range(SUBS):
            landed(h, n, 4)
            start(h, n, 6)

    for copy in a_copies:
        copy.wait_send()
    for copy in q_copies:
        copy.wait()
    weight_copy.wait()
    for h in range(2):
        for n in range(SUBS):
            for kind in (3, 5, 6):
                landed(h, n, kind)
    for h in range(2):
        for n in range(SUBS):
            for kind in range(KINDS):
                made[h, n, kind].wait_send()


def correlate_kernel(spectra, powers, flags, weights, vis, beam, col_scale, row_scale):
    feed = lax.axis_index("feed")
    c = pl.program_id(0)
    j = pl.program_id(1)

    @pl.when((c == 0) & (j == 0))
    def _():
        lane = lax.broadcasted_iota(jnp.int32, (CHAN_DEVS, 128), 1)
        power = jnp.zeros((CHAN_DEVS, 128), jnp.float32)
        for f in range(FEED_DEVS):
            power = jnp.where(lane // OWN == f, powers[f].reshape(CHAN_DEVS, 128), power)
        scale = lax.rsqrt(power / (BAND * NT) + EPSILON)
        col_scale[...] = scale * flags[...].astype(jnp.float32)
        for n in range(2):
            one = col_scale[pl.ds(2 * feed + n, 1), :] * (1.0 / NT)
            row_scale[128 * n : 128 * (n + 1), :] = jnp.broadcast_to(one, (128, 128)).T

    def parts(first, count):
        return jnp.concatenate(
            [
                spectra[h, pl.ds(first, count)].reshape(count * 128, 128)
                for h in range(2)
            ],
            axis=1,
        )

    def swapped(h):
        own = spectra[h, pl.ds(2 * feed, 2)].reshape(256, 128).astype(jnp.float32)
        lane = lax.broadcasted_iota(jnp.int32, (256, 128), 1)
        turned = pltpu.roll(own, HALF_T, 1)
        return jnp.where(lane < HALF_T, turned, -turned).astype(jnp.bfloat16)

    own = parts(2 * feed, 2)
    left = jnp.concatenate([own, jnp.concatenate([swapped(0), swapped(1)], axis=1)], axis=0)
    rows = row_scale[...]
    contract = (((1,), (1,)), ((), ()))
    tiles = vis.shape[3] // 256
    for n in range(tiles):
        right = parts(j * 2 * tiles + 2 * n, 2)
        both = lax.dot_general(left, right, contract, preferred_element_type=jnp.float32)
        for m in range(2):
            scale = rows * col_scale[pl.ds(j * 2 * tiles + 2 * n + m, 1), :]
            out = pl.ds((2 * n + m) * 128, 128)
            vis[0, 0, :, out] = both[0:256, 128 * m : 128 * (m + 1)] * scale
            vis[1, 0, :, out] = both[256:512, 128 * m : 128 * (m + 1)] * scale

    @pl.when(j == 0)
    def _():
        lane = lax.broadcasted_iota(jnp.int32, (OWN_BEAMS, 128), 1)
        halves = []
        for h in range(2):
            sums = jnp.dot(
                weights[...],
                spectra[h].reshape(INPUTS, 128),
                preferred_element_type=jnp.float32,
            )
            cos_part = sums[0:OWN_BEAMS]
            sin_part = pltpu.roll(sums[OWN_BEAMS : 2 * OWN_BEAMS], HALF_T, 1)
            field = cos_part + jnp.where(lane < HALF_T, -sin_part, sin_part)
            square = field * field
            halves.append(square + pltpu.roll(square, HALF_T, 1))
        power = jnp.where(lane < HALF_T, halves[0], halves[1]) * (1.0 / INPUTS)
        for n in range(PER_CHAN):

            @pl.when(c == n)
            def _():
                beam[:, n, :] = power


def on_device(table, raw_volts, channel_gains, feed_flags, steer_index):
    vmem = pl.BlockSpec(memory_space=pltpu.VMEM)
    hbm = pl.BlockSpec(memory_space=pl.ANY)
    bf16, f32 = jnp.bfloat16, jnp.float32
    dma = pltpu.SemaphoreType.DMA
    spectra, powers, weights = pl.pallas_call(
        turn_kernel,
        name="channelize_turn",
        out_shape=(
            jax.ShapeDtypeStruct((2, CHAN_DEVS, FEED_DEVS, UNIT, 128), bf16),
            jax.ShapeDtypeStruct((FEED_DEVS, CHAN_DEVS, 1, 128), f32),
            jax.ShapeDtypeStruct((2 * OWN_BEAMS, INPUTS), bf16),
        ),
        in_specs=[hbm, hbm, vmem, vmem, vmem],
        out_specs=(hbm, hbm, hbm),
        scratch_shapes=[
            pltpu.VMEM((SLABS * OWN, BLOCK), bf16),
            pltpu.VMEM((BLOCK, TAPS * 128), bf16),
            pltpu.VMEM((SLABS * OWN, TAPS * 128), f32),
            pltpu.VMEM((HALF_T * OWN, 128), f32),
            pltpu.VMEM((BAND * OWN, 128), f32),
            pltpu.VMEM((2, BAND * OWN, 128), bf16),
            pltpu.VMEM((128, 128), f32),
            pltpu.VMEM((8, 8, 128), f32),
            pltpu.VMEM((1, 128), f32),
            pltpu.VMEM((BEAMS, FEED_INPUTS), bf16),
            pltpu.VMEM((FEED_DEVS, OWN_BEAMS, FEED_INPUTS), bf16),
            pltpu.VMEM((2 * OWN_BEAMS, INPUTS), bf16),
            dma((4,)),
            dma,
            dma((3,)),
            dma((2, CHAN_DEVS)),
            dma((2, SUBS)),
            dma((2, KINDS, SUBS)),
            dma((2, KINDS, SUBS)),
            dma((FEED_DEVS,)),
            dma((FEED_DEVS,)),
            dma((CHAN_DEVS,)),
            dma((CHAN_DEVS,)),
            dma((FEED_DEVS,)),
            dma((FEED_DEVS,)),
            dma,
        ],
        compiler_params=pltpu.CompilerParams(
            collective_id=0, has_side_effects=True, vmem_limit_bytes=48 * 2**20
        ),
        cost_estimate=pl.CostEstimate(
            flops=2 * SLABS * OWN * BLOCK * 512, bytes_accessed=20_000_000, transcendentals=0
        ),
    )(raw_volts, table, channel_gains, steer_index, feed_flags.reshape(1, INPUTS))

    cols = 1024
    steps = INPUTS // cols
    visibility, beam_power = pl.pallas_call(
        correlate_kernel,
        name="correlate",
        grid=(PER_CHAN, steps),
        out_shape=(
            jax.ShapeDtypeStruct((2, PER_CHAN, FEED_INPUTS, INPUTS), f32),
            jax.ShapeDtypeStruct((OWN_BEAMS, PER_CHAN, NT), f32),
        ),
        in_specs=[
            pl.BlockSpec((2, CHAN_DEVS, FEED_DEVS, OWN, 128), lambda c, j: (0, 0, 0, c, 0)),
            pl.BlockSpec((FEED_DEVS, CHAN_DEVS, 1, 128), lambda c, j: (0, 0, 0, 0)),
            pl.BlockSpec((CHAN_DEVS, 128), lambda c, j: (0, 0)),
            pl.BlockSpec((2 * OWN_BEAMS, INPUTS), lambda c, j: (0, 0)),
        ],
        out_specs=(
            pl.BlockSpec((2, 1, FEED_INPUTS, cols), lambda c, j: (0, c, 0, j)),
            pl.BlockSpec((OWN_BEAMS, PER_CHAN, NT), lambda c, j: (0, 0, 0)),
        ),
        scratch_shapes=[pltpu.VMEM((CHAN_DEVS, 128), f32), pltpu.VMEM((256, 128), f32)],
        compiler_params=pltpu.CompilerParams(vmem_limit_bytes=48 * 2**20),
        cost_estimate=pl.CostEstimate(
            flops=2_700_000_000, bytes_accessed=22_000_000, transcendentals=0
        ),
    )(spectra, powers, feed_flags.reshape(CHAN_DEVS, 128), weights)
    return (visibility, beam_power)


def solution(mesh):
    table = filter_table()
    in_specs = (P(("chan", "feed"), None), P(None, None, ("chan", "feed")), P(), P(None, "feed"))
    out_specs = (P(None, "chan", "feed", None), P("feed", "chan", None))

    def body(raw_volts, channel_gains, feed_flags, steer_index):
        return on_device(
            jnp.asarray(table), raw_volts, channel_gains, feed_flags, steer_index
        )

    return jax.shard_map(
        body, mesh=mesh, in_specs=in_specs, out_specs=out_specs, check_vma=False
    )
```

time: 249 us -> 69.1 us (0.28)
  waiting for transfers between devices: 98.7 us -> 0 us
  Pallas kernels: 0 us -> 61.8 us
  blocking collectives: 47.1 us -> 0 us
  local copies, waits for them, and re-layouts: 42.6 us -> 6.32 us
  matrix products: 27.8 us -> 0 us
  other arithmetic: 17.2 us -> 0 us
  between operations: 15.1 us -> 0.67 us
    all_gather x1 -> x0, waiting for transfers between devices: 70.3 us -> none  [on_device(): grouped = lax.all_gather(sorted_chan, 'feed', axis=3, tiled=True)]
    pallas_call x0 -> x2, Pallas kernels: none -> 61.8 us  [the longest x1 51.2 us: on_device(): pl.pallas_call(turn_kernel, name='channelize_turn', out_shape=(jax.ShapeD...]
    psum x1 -> x0, blocking collectives: 29.9 us -> none  [on_device(): band_total = lax.psum(squared_sum(turned), 'chan')]
    reduce_scatter x1 -> x0, waiting for transfers between devices: 28.3 us -> none  [on_device(): lax.psum_scatter(jnp.stack([beam_re, beam_im], axis=1), 'feed', scatter_d...]
    dot_general x10 -> x0, matrix products: 27.8 us -> none  [the longest x4 15 us: channelize(): jnp.dot(frames, table[tap_index], preferred_element_type=jnp.float32)]
    slice x1 -> x0, local copies, waits for them, and re-layouts: 24.3 us -> none  [channelize(): blocks[:, tap_index:tap_index + spectra]]
    all_to_all x1 -> x0, blocking collectives: 17.2 us -> none  [on_device(): lax.all_to_all(local_spectra, 'chan', split_axis=0, concat_axis=3, tiled=...]
    reshape x1 -> x0, local copies, waits for them, and re-layouts: 12.7 us -> none  [channelize(): blocks = volt_rows.reshape(row_count, spectra + TAPS - 1, block_len)]
  transfers between devices with their start and end apart: 2 -> 0, of which waited for: 2 -> 0; matrix products, arithmetic and copies ran while one was open for 6% -> 0% of each run, Pallas kernels for 0% -> 0%
where the time goes in v1:
time: 69.1 us; the launch traced here: 68.8 us
  Pallas kernels  61.8 us (89%)
  local copies, waits for them, and re-layouts  6.32 us (9%)
    pallas_call x1, Pallas kernels, on_device(): pl.pallas_call(turn_kernel, name='channelize_turn', out_shape=(jax.ShapeD...  51.2 us
    pallas_call x1, Pallas kernels, on_device(): pl.pallas_call(correlate_kernel, name='correlate', grid=(PER_CHAN, steps)...  10.6 us
    unnamed x11, local copies, waits for them, and re-layouts  6.32 us

profile of v1, /device:TPU:0, one launch (start us, length us, event | category | flops | bytes accessed | tf_op | source)
XLA Modules:
  0.0 68.8 jit_solution(4002138997142105151)
XLA Ops:
  0.6 0.0 copy-start.2
  0.6 0.8 %copy.7.gains = f32[2,64,16]{2,1,0:T(8,128)S(1)} copy(f32[2,64,16]{1,2,0:T(8,128)} %param.6) | data formatting | bytes 16384 | tf_op args[1]
  1.4 0.0 copy-start
  1.4 1.0 %copy-done = s32[512,256]{1,0:T(8,128)S(1)} copy-done((s32[512,256]{1,0:T(8,128)S(1)}, s32[512,256]{1,0:T(8,128)}, u32[]{:S(2)}) %copy-start) | copy-done | bytes 524312
  2.5 0.0 copy-start.1
  2.5 0.7 %copy-done.1 = s32[2048]{0:T(1024)S(1)} copy-done((s32[2048]{0:T(1024)S(1)}, s32[2048]{0:T(1024)}, u32[]{:S(2)}) %copy-start.1) | copy-done | bytes 8216
  3.2 0.0 copy-start.3
  3.2 1.6 %copy-done.3 = bf16[2048,512]{1,0:T(8,128)(2,1)S(1)} copy-done((bf16[2048,512]{1,0:T(8,128)(2,1)S(1)}, bf16[2048,512]{1,0:T(8,128)(2,1)}, u32[]{:S(2)}) %copy-start.3) | copy-done | bytes 2097176
  4.8 51.2 %channelize_turn.1 = (bf16[2,16,8,64,128]{4,3,2,1,0:T(8,128)(2,1)}, f32[8,16,1,128]{3,2,1,0:T(1,128)S(1)}, bf16[128,2048]{1,0:T(8,128)(2,1)S(1)}) custom-call(bf16[16,268288]{1,0:T(8,128)(2,1)} %raw.1, bf16[2048,512]{1,0:T(8,128)(2,1)S(1)} %copy-done.3, f32[2,64,16]{2,1,0:T(8,128)S(1)} %copy.7.gains, s32[512,256]{1,0:T(8,128)S(1)} %copy-done, ...), custom_call_target="tpu_custom_call" | custom-call | flops 4395630592 | bytes 20000000 | tf_op jit(solution)/shard_map/channelize_turn/pallas_call | solution.py:434
  56.0 0.0 copy-done.2
  56.0 0.0 copy-start.4
  56.0 2.2 %copy-done.4 = bf16[2,16,8,64,128]{4,3,2,1,0:T(8,128)(2,1)S(1)} copy-done((bf16[2,16,8,64,128]{4,3,2,1,0:T(8,128)(2,1)S(1)}, bf16[2,16,8,64,128]{4,3,2,1,0:T(8,128)(2,1)}, u32[]{:S(2)}) %copy-start.4) | copy-done | bytes 4194328
  58.2 10.6 %correlate.1 = (f32[2,4,256,2048]{3,2,1,0:T(8,128)}, f32[64,4,128]{2,1,0:T(4,128)}) custom-call(bf16[2,16,8,64,128]{4,3,2,1,0:T(8,128)(2,1)S(1)} %copy-done.4, f32[8,16,1,128]{3,2,1,0:T(1,128)S(1)} %get-tuple-element.6.powers, s32[16,128]{1,0:T(8,128)S(1)} %bitcast.3, bf16[128,2048]{1,0:T(8,128)(2,1)S(1)} %get-tuple-element.7.weights), custom_call_target="tpu_custom_call" | custom-call | flops 2700000000 | bytes 22000000 | tf_op jit(solution)/shard_map/correlate/pallas_call | solution.py:482
Async XLA Ops:
  0.6 55.4 %copy-start.2 = (s32[2048]{0:T(1024)S(1)}, s32[2048]{0:T(1024)}, u32[]{:S(2)}) copy-start(s32[2048]{0:T(1024)} %param.7) | copy-start | bytes 24580
  1.4 1.0 %copy-start = (s32[512,256]{1,0:T(8,128)S(1)}, s32[512,256]{1,0:T(8,128)}, u32[]{:S(2)}) copy-start(s32[512,256]{1,0:T(8,128)} %steer.1) | copy-start | bytes 1572868
  2.5 0.7 %copy-start.1 = (s32[2048]{0:T(1024)S(1)}, s32[2048]{0:T(1024)}, u32[]{:S(2)}) copy-start(s32[2048]{0:T(1024)} %param.7) | copy-start | bytes 24580
  3.2 1.6 %copy-start.3 = (bf16[2048,512]{1,0:T(8,128)(2,1)S(1)}, bf16[2048,512]{1,0:T(8,128)(2,1)}, u32[]{:S(2)}) copy-start(bf16[2048,512]{1,0:T(8,128)(2,1)} %constant.2.clone.table) | copy-start | bytes 6291460
  56.0 2.2 %copy-start.4 = (bf16[2,16,8,64,128]{4,3,2,1,0:T(8,128)(2,1)S(1)}, bf16[2,16,8,64,128]{4,3,2,1,0:T(8,128)(2,1)}, u32[]{:S(2)}) copy-start(bf16[2,16,8,64,128]{4,3,2,1,0:T(8,128)(2,1)} %get-tuple-element.5.spectra) | copy-start | bytes 12582916

commit v2 on v1

--- a/solution.py
+++ b/solution.py
@@ -30,8 +30,9 @@
 SUB = CHAN_DEVS // SUBS
 OWN_BEAMS = BEAMS // FEED_DEVS
 FEED_INPUTS = INPUTS // FEED_DEVS
-KINDS = 7
-FIRST_SLABS = 68
+KINDS = 6
+OUT_PARTS = 4
+IN_PARTS = 1
 MESH = pl.DeviceIdType.MESH
 
 
@@ -51,9 +52,9 @@
 
 def turn_kernel(
     raw, table, gains, steer, flags, spectra, powers, weights,
-    volts, tab, conv, summed, turned, outbox, gain_sq, power_acc, power_row,
+    volts, tab, conv, summed, turned, outbox, gain_buf, steer_buf, flag_buf, power_acc, power_row,
     steer_out, steer_in, weight_buf,
-    load_sem, tab_sem, own_sem, a_send, a_recv, b_send, b_recv,
+    load_sem, tab_sem, small_sem, own_sem, a_send, a_recv, b_send, b_recv,
     s_send, s_recv, p_send, p_recv, q_send, q_recv, out_sem,
 ):
     chan = lax.axis_index("chan")
@@ -70,17 +71,39 @@
     over = (chan, feed_at(0, True))
 
     barrier = pltpu.get_barrier_semaphore()
-    for d in range(1, CHAN_DEVS):
+    plane = [
+        ((half, d), across)
+        for half in range(SUBS)
+        for across in range(2)
+        for d in range(SUB)
+        if (half, d, across) != (0, 0, 0)
+    ]
+
+    def plane_peer(half, d):
+        first = (chan // SUB + half) % SUBS * SUB
+        return first + lax.rem(chan + d, SUB)
+
+    distant = [(dx, across) for dx in (1, 3, 2) for across in (False, True)]
+    for (half, d), across in plane:
         pl.semaphore_signal(
-            barrier, inc=1, device_id=(lax.rem(chan + d, CHAN_DEVS), feed), device_id_type=MESH
-        )
-    for d in range(1, FEED_DEVS):
+            barrier,
+            inc=1,
+            device_id=(plane_peer(half, d), feed_at(0, bool(across))),
+            device_id_type=MESH,
+        )
+    for dx, across in distant:
         pl.semaphore_signal(
-            barrier, inc=1, device_id=(chan, lax.rem(feed + d, FEED_DEVS)), device_id_type=MESH
+            barrier, inc=1, device_id=(chan, feed_at(dx, across)), device_id_type=MESH
         )
 
     tab_copy = pltpu.make_async_copy(table, tab, tab_sem)
     tab_copy.start()
+    gain_copy = pltpu.make_async_copy(gains, gain_buf, small_sem.at[0])
+    gain_copy.start()
+    steer_copy = pltpu.make_async_copy(steer, steer_buf, small_sem.at[1])
+    steer_copy.start()
+    flag_copy = pltpu.make_async_copy(flags, flag_buf, small_sem.at[2])
+    flag_copy.start()
     groups = [(0, 34), (34, 34), (68, 32), (100, 31)]
     for g, (first, count) in enumerate(groups):
 
@@ -93,19 +116,16 @@
                 load_sem.at[g],
             ).start()
 
-    steer_out[...] = steer[...].astype(jnp.float32).astype(jnp.bfloat16)
-
-    gain_sq[...] = jnp.zeros_like(gain_sq)
-    gain_sq[0:BAND, 0:OWN] = gains[0]
-    gain_sq[BAND : 2 * BAND, 0:OWN] = gains[1]
-    gain_rows = gain_sq[...].T[0:OWN]
+    steer_copy.wait()
+    steer_out[...] = steer_buf[...].astype(jnp.float32).astype(jnp.bfloat16)
+
+    gain_copy.wait()
+    pair_re = jnp.concatenate([gain_buf[0, 0:8], gain_buf[0, 8:16]], axis=1)
+    pair_im = jnp.concatenate([gain_buf[1, 0:8], gain_buf[1, 8:16]], axis=1)
     lane8 = lax.broadcasted_iota(jnp.int32, (8, 128), 1)
     low8 = lane8 < BAND
-    g_lo, g_hi = gain_rows[0:8], gain_rows[8:16]
-    pair_re = jnp.where(low8, g_lo, pltpu.roll(g_hi, BAND, 1))
-    pair_im = jnp.where(low8, pltpu.roll(g_lo, BAND, 1), g_hi)
-
-    pl.semaphore_wait(barrier, CHAN_DEVS + FEED_DEVS - 2)
+
+    pl.semaphore_wait(barrier, len(plane) + len(distant))
 
     steer_copies = []
     for d in range(1, FEED_DEVS):
@@ -175,23 +195,24 @@
             own_sem.at[h],
         )
         mine.start()
-        for d in range(1, CHAN_DEVS):
-            other = lax.rem(chan + d, CHAN_DEVS)
+        for n, ((half, d), across) in enumerate(plane):
+            other = plane_peer(half, d)
             copy = pltpu.make_async_remote_copy(
                 src_ref=outbox.at[h, pl.ds(pl.multiple_of(other * UNIT, UNIT), UNIT), :],
                 dst_ref=spectra.at[h, chan, feed],
-                send_sem=a_send.at[h, d],
-                recv_sem=a_recv.at[h, chan // SUB],
-                device_id=(other, feed),
+                send_sem=a_send.at[h, n],
+                recv_sem=a_recv.at[h, across, half],
+                device_id=(other, feed_at(0, bool(across))),
                 device_id_type=MESH,
             )
             copy.start()
             a_copies.append(copy)
         return mine
 
-    def arrived(h, sub, count):
+    def arrived(h, across, half):
+        count = SUB - 1 if (across, half) == (0, 0) else SUB
         rows = spectra.at[h, pl.ds(0, count), 0]
-        pltpu.make_async_copy(rows, rows, a_recv.at[h, sub]).wait()
+        pltpu.make_async_copy(rows, rows, a_recv.at[h, across, half]).wait()
 
     sub_of = [chan // SUB, 1 - chan // SUB]
 
@@ -207,25 +228,24 @@
         )
 
     plans = []
-    for h in range(2):
-        fore, back = (right, left) if h == 0 else (left, right)
-        s = 1 if h == 0 else -1
+    for n in range(SUBS):
+        fore, back, s = (right, left, 1) if n == 0 else (left, right, -1)
         plans.append(
-            [
-                (feed, fore),
-                (feed, back),
-                (feed, over),
-                (feed_at(-s, False), fore),
-                (feed_at(s, False), over),
-                (feed_at(0, True), fore),
-                (feed_at(s, True), back),
-            ]
-        )
+            {
+                "own fore": (feed, fore),
+                "own back": (feed, back),
+                "pass fore": (feed_at(-s, False), fore),
+                "pass over": (feed_at(s, False), over),
+                "other fore": (feed_at(0, True), fore),
+                "other back": (feed_at(s, True), back),
+            }
+        )
+    kinds = list(plans[0])
     made = {}
 
     def start(h, n, kind):
-        origin, target = plans[h][kind]
-        made[h, n, kind] = spread(h, n, kind, origin, target)
+        origin, target = plans[n][kind]
+        made[h, n, kind] = spread(h, n, kinds.index(kind), origin, target)
         made[h, n, kind].start()
 
     def landed(h, n, kind):
@@ -234,11 +254,21 @@
     def step_one(h, n, mine):
         if n == 0:
             mine.wait()
-            arrived(h, sub_of[0], SUB - 1)
-        else:
-            arrived(h, sub_of[1], SUB)
-        for kind in (2, 0, 1):
-            start(h, n, kind)
+        arrived(h, 0, n)
+        start(h, n, "own back")
+        start(h, n, "own fore")
+        arrived(h, 1, n)
+        start(h, n, "other fore")
+
+    def step_two(h, n):
+        landed(h, n, "own back")
+        start(h, n, "pass over")
+        landed(h, n, "own fore")
+        start(h, n, "pass fore")
+
+    def step_three(h, n):
+        landed(h, n, "pass over")
+        start(h, n, "other back")
 
     loaded(0)
     tab_copy.wait()
@@ -286,6 +316,7 @@
     for copy in steer_copies:
         copy.wait()
     own_steer.wait()
+    flag_copy.wait()
     for g in range(FEED_DEVS):
         cols = pl.ds(g * FEED_INPUTS, FEED_INPUTS)
         index = steer_in[g].astype(jnp.float32)
@@ -301,25 +332,20 @@
         sin_neg = (quarter == 2.0) | (quarter == 3.0)
         cos_mag = jnp.where(swap, sin, cos)
         sin_mag = jnp.where(swap, cos, sin)
-        good = flags[:, cols].astype(jnp.float32)
+        good = flag_buf[:, cols].astype(jnp.float32)
         weight_buf[0:OWN_BEAMS, cols] = (jnp.where(cos_neg, -cos_mag, cos_mag) * good).astype(
             jnp.bfloat16
         )
         weight_buf[OWN_BEAMS : 2 * OWN_BEAMS, cols] = (
             jnp.where(sin_neg, -sin_mag, sin_mag) * good
         ).astype(jnp.bfloat16)
+
     weight_copy = pltpu.make_async_copy(weight_buf, weights, out_sem)
     weight_copy.start()
 
     for h in range(2):
-        fore_in, back_in = 0, 1
         for n in range(SUBS):
-            landed(h, n, back_in)
-            start(h, n, 4)
-            landed(h, n, fore_in)
-            start(h, n, 3)
-            landed(h, n, 2)
-            start(h, n, 5)
+            step_two(h, n)
 
     p_own.wait()
     for copy in p_copies:
@@ -339,8 +365,7 @@
 
     for h in range(2):
         for n in range(SUBS):
-            landed(h, n, 4)
-            start(h, n, 6)
+            step_three(h, n)
 
     for copy in a_copies:
         copy.wait_send()
@@ -349,85 +374,122 @@
     weight_copy.wait()
     for h in range(2):
         for n in range(SUBS):
-            for kind in (3, 5, 6):
+            for kind in ("other fore", "pass fore", "other back"):
                 landed(h, n, kind)
-    for h in range(2):
-        for n in range(SUBS):
-            for kind in range(KINDS):
-                made[h, n, kind].wait_send()
-
-
-def correlate_kernel(spectra, powers, flags, weights, vis, beam, col_scale, row_scale):
+    for copy in made.values():
+        copy.wait_send()
+
+
+def correlate_kernel(
+    spectra, powers, flags, weights, vis, beam,
+    block, power_buf, flag_buf, weight_buf, product, col_scale, row_scale,
+    in_sem, small_sem, out_sem,
+):
     feed = lax.axis_index("feed")
-    c = pl.program_id(0)
-    j = pl.program_id(1)
-
-    @pl.when((c == 0) & (j == 0))
-    def _():
-        lane = lax.broadcasted_iota(jnp.int32, (CHAN_DEVS, 128), 1)
-        power = jnp.zeros((CHAN_DEVS, 128), jnp.float32)
-        for f in range(FEED_DEVS):
-            power = jnp.where(lane // OWN == f, powers[f].reshape(CHAN_DEVS, 128), power)
-        scale = lax.rsqrt(power / (BAND * NT) + EPSILON)
-        col_scale[...] = scale * flags[...].astype(jnp.float32)
-        for n in range(2):
-            one = col_scale[pl.ds(2 * feed + n, 1), :] * (1.0 / NT)
-            row_scale[128 * n : 128 * (n + 1), :] = jnp.broadcast_to(one, (128, 128)).T
-
-    def parts(first, count):
+    power_copy = pltpu.make_async_copy(powers, power_buf, small_sem.at[0])
+    flag_copy = pltpu.make_async_copy(flags, flag_buf, small_sem.at[1])
+    weight_copy = pltpu.make_async_copy(weights, weight_buf, small_sem.at[2])
+
+    def loads(c):
+        rows = pl.ds(pl.multiple_of(c * OWN, OWN), OWN)
+        step = CHAN_DEVS // IN_PARTS
+        return [
+            pltpu.make_async_copy(
+                spectra.at[h, pl.ds(n * step, step), :, rows, :],
+                block.at[c, h, pl.ds(n * step, step)],
+                in_sem.at[c],
+            )
+            for n in range(IN_PARTS)
+            for h in range(2)
+        ]
+
+    power_copy.start()
+    flag_copy.start()
+    for c in range(PER_CHAN):
+        for copy in loads(c):
+            copy.start()
+    weight_copy.start()
+    power_copy.wait()
+    flag_copy.wait()
+    lane = lax.broadcasted_iota(jnp.int32, (CHAN_DEVS, 128), 1)
+    power = jnp.zeros((CHAN_DEVS, 128), jnp.float32)
+    for f in range(FEED_DEVS):
+        power = jnp.where(lane // OWN == f, power_buf[f].reshape(CHAN_DEVS, 128), power)
+    scale = lax.rsqrt(power / (BAND * NT) + EPSILON)
+    col_scale[...] = scale * flag_buf[...].astype(jnp.float32)
+    for n in range(2):
+        one = col_scale[pl.ds(2 * feed + n, 1), :] * (1.0 / NT)
+        row_scale[128 * n : 128 * (n + 1), :] = jnp.broadcast_to(one, (128, 128)).T
+
+    def parts(c, first, count):
         return jnp.concatenate(
-            [
-                spectra[h, pl.ds(first, count)].reshape(count * 128, 128)
-                for h in range(2)
-            ],
+            [block[c, h, pl.ds(first, count)].reshape(count * 128, 128) for h in range(2)],
             axis=1,
         )
 
-    def swapped(h):
-        own = spectra[h, pl.ds(2 * feed, 2)].reshape(256, 128).astype(jnp.float32)
+    def swapped(c, h):
+        own = block[c, h, pl.ds(2 * feed, 2)].reshape(256, 128).astype(jnp.float32)
         lane = lax.broadcasted_iota(jnp.int32, (256, 128), 1)
         turned = pltpu.roll(own, HALF_T, 1)
         return jnp.where(lane < HALF_T, turned, -turned).astype(jnp.bfloat16)
 
-    own = parts(2 * feed, 2)
-    left = jnp.concatenate([own, jnp.concatenate([swapped(0), swapped(1)], axis=1)], axis=0)
-    rows = row_scale[...]
-    contract = (((1,), (1,)), ((), ()))
-    tiles = vis.shape[3] // 256
-    for n in range(tiles):
-        right = parts(j * 2 * tiles + 2 * n, 2)
-        both = lax.dot_general(left, right, contract, preferred_element_type=jnp.float32)
-        for m in range(2):
-            scale = rows * col_scale[pl.ds(j * 2 * tiles + 2 * n + m, 1), :]
-            out = pl.ds((2 * n + m) * 128, 128)
-            vis[0, 0, :, out] = both[0:256, 128 * m : 128 * (m + 1)] * scale
-            vis[1, 0, :, out] = both[256:512, 128 * m : 128 * (m + 1)] * scale
-
-    @pl.when(j == 0)
-    def _():
-        lane = lax.broadcasted_iota(jnp.int32, (OWN_BEAMS, 128), 1)
+    def stores(c):
+        copies = []
+        step = FEED_INPUTS // OUT_PARTS
+        for p in range(2):
+            for n in range(OUT_PARTS):
+                rows = pl.ds(n * step, step)
+                copies.append(
+                    pltpu.make_async_copy(
+                        product.at[p, c, rows, :], vis.at[p, c, rows, :], out_sem.at[c]
+                    )
+                )
+        return copies
+
+    @pl.loop(0, PER_CHAN)
+    def _(c):
+        pltpu.make_async_copy(block.at[c], block.at[c], in_sem.at[c]).wait()
+
+        own = parts(c, 2 * feed, 2)
+        turned = jnp.concatenate([swapped(c, 0), swapped(c, 1)], axis=1)
+        left = jnp.concatenate([own, turned], axis=0)
+        rows = row_scale[...]
+        for n in range(INPUTS // 256):
+            both = lax.dot_general(
+                left,
+                parts(c, 2 * n, 2),
+                (((1,), (1,)), ((), ())),
+                preferred_element_type=jnp.float32,
+            )
+            for m in range(2):
+                scale = rows * col_scale[2 * n + m : 2 * n + m + 1, :]
+                out = pl.ds((2 * n + m) * 128, 128)
+                product[0, c, :, out] = both[0:256, 128 * m : 128 * (m + 1)] * scale
+                product[1, c, :, out] = both[256:512, 128 * m : 128 * (m + 1)] * scale
+        for copy in stores(c):
+            copy.start()
+
+    weight_copy.wait()
+    lane = lax.broadcasted_iota(jnp.int32, (OWN_BEAMS, 128), 1)
+    for c in range(PER_CHAN):
+        sums = jnp.dot(
+            weight_buf[...], parts(c, 0, CHAN_DEVS), preferred_element_type=jnp.float32
+        )
         halves = []
         for h in range(2):
-            sums = jnp.dot(
-                weights[...],
-                spectra[h].reshape(INPUTS, 128),
-                preferred_element_type=jnp.float32,
-            )
-            cos_part = sums[0:OWN_BEAMS]
-            sin_part = pltpu.roll(sums[OWN_BEAMS : 2 * OWN_BEAMS], HALF_T, 1)
+            cols = slice(128 * h, 128 * (h + 1))
+            cos_part = sums[0:OWN_BEAMS, cols]
+            sin_part = pltpu.roll(sums[OWN_BEAMS : 2 * OWN_BEAMS, cols], HALF_T, 1)
             field = cos_part + jnp.where(lane < HALF_T, -sin_part, sin_part)
             square = field * field
             halves.append(square + pltpu.roll(square, HALF_T, 1))
-        power = jnp.where(lane < HALF_T, halves[0], halves[1]) * (1.0 / INPUTS)
-        for n in range(PER_CHAN):
-
-            @pl.when(c == n)
-            def _():
-                beam[:, n, :] = power
-
-
-def on_device(table, raw_volts, channel_gains, feed_flags, steer_index):
-    vmem = pl.BlockSpec(memory_space=pltpu.VMEM)
+        beam[:, c, :] = jnp.where(lane < HALF_T, halves[0], halves[1]) * (1.0 / INPUTS)
+    for c in range(PER_CHAN):
+        whole = product.at[:, c]
+        pltpu.make_async_copy(whole, whole, out_sem.at[c]).wait()
+
+
+def channelize_turn(table, raw_volts, channel_gains, feed_flags, steer_index):
     hbm = pl.BlockSpec(memory_space=pl.ANY)
     bf16, f32 = jnp.bfloat16, jnp.float32
     dma = pltpu.SemaphoreType.DMA
@@ -439,7 +501,7 @@
             jax.ShapeDtypeStruct((FEED_DEVS, CHAN_DEVS, 1, 128), f32),
             jax.ShapeDtypeStruct((2 * OWN_BEAMS, INPUTS), bf16),
         ),
-        in_specs=[hbm, hbm, vmem, vmem, vmem],
+        in_specs=[hbm] * 5,
         out_specs=(hbm, hbm, hbm),
         scratch_shapes=[
             pltpu.VMEM((SLABS * OWN, BLOCK), bf16),
@@ -448,7 +510,9 @@
             pltpu.VMEM((HALF_T * OWN, 128), f32),
             pltpu.VMEM((BAND * OWN, 128), f32),
             pltpu.VMEM((2, BAND * OWN, 128), bf16),
-            pltpu.VMEM((128, 128), f32),
+            pltpu.VMEM((2, OWN, BAND), f32),
+            pltpu.VMEM((BEAMS, FEED_INPUTS), jnp.int32),
+            pltpu.VMEM((1, INPUTS), jnp.int32),
             pltpu.VMEM((8, 8, 128), f32),
             pltpu.VMEM((1, 128), f32),
             pltpu.VMEM((BEAMS, FEED_INPUTS), bf16),
@@ -457,8 +521,9 @@
             dma((4,)),
             dma,
             dma((3,)),
-            dma((2, CHAN_DEVS)),
-            dma((2, SUBS)),
+            dma((3,)),
+            dma((2, 2 * CHAN_DEVS)),
+            dma((2, 2, SUBS)),
             dma((2, KINDS, SUBS)),
             dma((2, KINDS, SUBS)),
             dma((FEED_DEVS,)),
@@ -470,40 +535,46 @@
             dma,
         ],
         compiler_params=pltpu.CompilerParams(
-            collective_id=0, has_side_effects=True, vmem_limit_bytes=48 * 2**20
+            collective_id=0, has_side_effects=True, vmem_limit_bytes=60 * 2**20
         ),
         cost_estimate=pl.CostEstimate(
             flops=2 * SLABS * OWN * BLOCK * 512, bytes_accessed=20_000_000, transcendentals=0
         ),
-    )(raw_volts, table, channel_gains, steer_index, feed_flags.reshape(1, INPUTS))
-
-    cols = 1024
-    steps = INPUTS // cols
-    visibility, beam_power = pl.pallas_call(
+    )(raw_volts, table, jnp.transpose(channel_gains, (0, 2, 1)), steer_index, feed_flags.reshape(1, INPUTS))
+    return spectra, powers, weights
+
+
+def correlate(spectra, powers, feed_flags, weights):
+    bf16, f32 = jnp.bfloat16, jnp.float32
+    hbm = pl.BlockSpec(memory_space=pl.ANY)
+    vmem = pl.BlockSpec(memory_space=pltpu.VMEM)
+    dma = pltpu.SemaphoreType.DMA
+    return pl.pallas_call(
         correlate_kernel,
         name="correlate",
-        grid=(PER_CHAN, steps),
         out_shape=(
             jax.ShapeDtypeStruct((2, PER_CHAN, FEED_INPUTS, INPUTS), f32),
             jax.ShapeDtypeStruct((OWN_BEAMS, PER_CHAN, NT), f32),
         ),
-        in_specs=[
-            pl.BlockSpec((2, CHAN_DEVS, FEED_DEVS, OWN, 128), lambda c, j: (0, 0, 0, c, 0)),
-            pl.BlockSpec((FEED_DEVS, CHAN_DEVS, 1, 128), lambda c, j: (0, 0, 0, 0)),
-            pl.BlockSpec((CHAN_DEVS, 128), lambda c, j: (0, 0)),
-            pl.BlockSpec((2 * OWN_BEAMS, INPUTS), lambda c, j: (0, 0)),
+        in_specs=[hbm] * 4,
+        out_specs=(hbm, vmem),
+        scratch_shapes=[
+            pltpu.VMEM((PER_CHAN, 2, CHAN_DEVS, FEED_DEVS, OWN, 128), bf16),
+            pltpu.VMEM((FEED_DEVS, CHAN_DEVS, 1, 128), f32),
+            pltpu.VMEM((CHAN_DEVS, 128), jnp.int32),
+            pltpu.VMEM((2 * OWN_BEAMS, INPUTS), bf16),
+            pltpu.VMEM((2, PER_CHAN, FEED_INPUTS, INPUTS), f32),
+            pltpu.VMEM((CHAN_DEVS, 128), f32),
+            pltpu.VMEM((256, 128), f32),
+            dma((PER_CHAN,)),
+            dma((3,)),
+            dma((PER_CHAN,)),
         ],
-        out_specs=(
-            pl.BlockSpec((2, 1, FEED_INPUTS, cols), lambda c, j: (0, c, 0, j)),
-            pl.BlockSpec((OWN_BEAMS, PER_CHAN, NT), lambda c, j: (0, 0, 0)),
-        ),
-        scratch_shapes=[pltpu.VMEM((CHAN_DEVS, 128), f32), pltpu.VMEM((256, 128), f32)],
-        compiler_params=pltpu.CompilerParams(vmem_limit_bytes=48 * 2**20),
+        compiler_params=pltpu.CompilerParams(vmem_limit_bytes=60 * 2**20),
         cost_estimate=pl.CostEstimate(
             flops=2_700_000_000, bytes_accessed=22_000_000, transcendentals=0
         ),
     )(spectra, powers, feed_flags.reshape(CHAN_DEVS, 128), weights)
-    return (visibility, beam_power)
 
 
 def solution(mesh):
@@ -512,9 +583,10 @@
     out_specs = (P(None, "chan", "feed", None), P("feed", "chan", None))
 
     def body(raw_volts, channel_gains, feed_flags, steer_index):
-        return on_device(
+        spectra, powers, weights = channelize_turn(
             jnp.asarray(table), raw_volts, channel_gains, feed_flags, steer_index
         )
+        return correlate(spectra, powers, feed_flags, weights)
 
     return jax.shard_map(
         body, mesh=mesh, in_specs=in_specs, out_specs=out_specs, check_vma=False

time: 69.1 us -> 59.8 us (0.87)
  local copies, waits for them, and re-layouts: 6.32 us -> 0 us
  Pallas kernels: 61.8 us -> 58.7 us
    unnamed x11 -> x0, local copies, waits for them, and re-layouts: 6.32 us -> none
    pallas_call x2, Pallas kernels: 61.8 us -> 58.7 us  [the longest x1 49.5 us: channelize_turn(): pl.pallas_call(turn_kernel, name='channelize_turn', out_shape=(jax.ShapeD...]
where the time goes in v2:
time: 59.8 us; the launch traced here: 59.3 us
  Pallas kernels  58.7 us (98%)
  between operations  0.64 us (1%)
    pallas_call x1, Pallas kernels, channelize_turn(): pl.pallas_call(turn_kernel, name='channelize_turn', out_shape=(jax.ShapeD...  49.5 us
    pallas_call x1, Pallas kernels, correlate(): pl.pallas_call(correlate_kernel, name='correlate', out_shape=(jax.ShapeDt...  9.15 us

profile of v2, /device:TPU:0, one launch (start us, length us, event | category | flops | bytes accessed | tf_op | source)
XLA Modules:
  0.0 59.3 jit_solution(6962863315140723591)
XLA Ops:
  0.6 49.5 %channelize_turn.1 = (bf16[2,16,8,64,128]{4,3,2,1,0:T(8,128)(2,1)}, f32[8,16,1,128]{3,2,1,0:T(1,128)}, bf16[128,2048]{1,0:T(8,128)(2,1)}) custom-call(bf16[16,268288]{1,0:T(8,128)(2,1)} %raw.1, bf16[2048,512]{1,0:T(8,128)(2,1)} %constant.2.clone.table, f32[2,16,64]{2,1,0:T(8,128)} %bitcast.3, s32[512,256]{1,0:T(8,128)} %steer.1, s32[1,2048]{1,0:T(1,128)} %bitcast.4), custom_call_target="tpu_custom_call" | custom-call | flops 4395630592 | bytes 20000000 | tf_op jit(solution)/shard_map/channelize_turn/pallas_call | solution.py:496
  50.2 9.2 %correlate.1 = (f32[2,4,256,2048]{3,2,1,0:T(8,128)}, f32[64,4,128]{2,1,0:T(4,128)}) custom-call(bf16[2,16,8,64,128]{4,3,2,1,0:T(8,128)(2,1)} %get-tuple-element.5.spectra, f32[8,16,1,128]{3,2,1,0:T(1,128)} %get-tuple-element.6.powers, s32[16,128]{1,0:T(8,128)} %bitcast.5, bf16[128,2048]{1,0:T(8,128)(2,1)} %get-tuple-element.7.weights), custom_call_target="tpu_custom_call" | custom-call | flops 2700000000 | bytes 22000000 | tf_op jit(solution)/shard_map/correlate/pallas_call | solution.py:552

commit v3 on v2

--- a/solution.py
+++ b/solution.py
@@ -32,7 +32,6 @@
 FEED_INPUTS = INPUTS // FEED_DEVS
 KINDS = 6
 OUT_PARTS = 4
-IN_PARTS = 1
 MESH = pl.DeviceIdType.MESH
 
 
@@ -51,8 +50,8 @@
 
 
 def turn_kernel(
-    raw, table, gains, steer, flags, spectra, powers, weights,
-    volts, tab, conv, summed, turned, outbox, gain_buf, steer_buf, flag_buf, power_acc, power_row,
+    raw, table, gains, steer, spectra, powers, weights,
+    volts, tab, conv, summed, turned, outbox, gain_buf, steer_buf, power_acc, power_row,
     steer_out, steer_in, weight_buf,
     load_sem, tab_sem, small_sem, own_sem, a_send, a_recv, b_send, b_recv,
     s_send, s_recv, p_send, p_recv, q_send, q_recv, out_sem,
@@ -96,14 +95,12 @@
             barrier, inc=1, device_id=(chan, feed_at(dx, across)), device_id_type=MESH
         )
 
-    tab_copy = pltpu.make_async_copy(table, tab, tab_sem)
+    tab_copy = pltpu.make_async_copy(table.at[0], tab, tab_sem)
     tab_copy.start()
     gain_copy = pltpu.make_async_copy(gains, gain_buf, small_sem.at[0])
     gain_copy.start()
     steer_copy = pltpu.make_async_copy(steer, steer_buf, small_sem.at[1])
     steer_copy.start()
-    flag_copy = pltpu.make_async_copy(flags, flag_buf, small_sem.at[2])
-    flag_copy.start()
     groups = [(0, 34), (34, 34), (68, 32), (100, 31)]
     for g, (first, count) in enumerate(groups):
 
@@ -116,37 +113,11 @@
                 load_sem.at[g],
             ).start()
 
-    steer_copy.wait()
-    steer_out[...] = steer_buf[...].astype(jnp.float32).astype(jnp.bfloat16)
-
     gain_copy.wait()
     pair_re = jnp.concatenate([gain_buf[0, 0:8], gain_buf[0, 8:16]], axis=1)
     pair_im = jnp.concatenate([gain_buf[1, 0:8], gain_buf[1, 8:16]], axis=1)
     lane8 = lax.broadcasted_iota(jnp.int32, (8, 128), 1)
     low8 = lane8 < BAND
-
-    pl.semaphore_wait(barrier, len(plane) + len(distant))
-
-    steer_copies = []
-    for d in range(1, FEED_DEVS):
-        other = lax.rem(feed + d, FEED_DEVS)
-        steer_copies.append(
-            pltpu.make_async_remote_copy(
-                src_ref=steer_out.at[pl.ds(pl.multiple_of(other * OWN_BEAMS, OWN_BEAMS), OWN_BEAMS), :],
-                dst_ref=steer_in.at[feed],
-                send_sem=s_send.at[d],
-                recv_sem=s_recv.at[d],
-                device_id=(chan, other),
-                device_id_type=MESH,
-            )
-        )
-        steer_copies[-1].start()
-    own_steer = pltpu.make_async_copy(
-        steer_out.at[pl.ds(pl.multiple_of(feed * OWN_BEAMS, OWN_BEAMS), OWN_BEAMS), :],
-        steer_in.at[feed],
-        s_send.at[0],
-    )
-    own_steer.start()
 
     low = lax.broadcasted_iota(jnp.int32, (HALF_T, 128), 1) < BAND
 
@@ -273,6 +244,31 @@
     loaded(0)
     tab_copy.wait()
     convolve(0, 34)
+
+    steer_copy.wait()
+    steer_out[...] = steer_buf[...].astype(jnp.float32).astype(jnp.bfloat16)
+    pl.semaphore_wait(barrier, len(plane) + len(distant))
+    steer_copies = []
+    for d in range(1, FEED_DEVS):
+        other = lax.rem(feed + d, FEED_DEVS)
+        steer_copies.append(
+            pltpu.make_async_remote_copy(
+                src_ref=steer_out.at[pl.ds(pl.multiple_of(other * OWN_BEAMS, OWN_BEAMS), OWN_BEAMS), :],
+                dst_ref=steer_in.at[feed],
+                send_sem=s_send.at[d],
+                recv_sem=s_recv.at[d],
+                device_id=(chan, other),
+                device_id_type=MESH,
+            )
+        )
+        steer_copies[-1].start()
+    own_steer = pltpu.make_async_copy(
+        steer_out.at[pl.ds(pl.multiple_of(feed * OWN_BEAMS, OWN_BEAMS), OWN_BEAMS), :],
+        steer_in.at[feed],
+        s_send.at[0],
+    )
+    own_steer.start()
+
     loaded(1)
     convolve(34, 34)
     turn(0)
@@ -310,13 +306,14 @@
         copy.start()
         p_copies.append(copy)
 
+    step_two(0, 0)
     step_one(1, 0, mine1)
+    step_two(0, 1)
     step_one(1, 1, mine1)
 
     for copy in steer_copies:
         copy.wait()
     own_steer.wait()
-    flag_copy.wait()
     for g in range(FEED_DEVS):
         cols = pl.ds(g * FEED_INPUTS, FEED_INPUTS)
         index = steer_in[g].astype(jnp.float32)
@@ -332,20 +329,16 @@
         sin_neg = (quarter == 2.0) | (quarter == 3.0)
         cos_mag = jnp.where(swap, sin, cos)
         sin_mag = jnp.where(swap, cos, sin)
-        good = flag_buf[:, cols].astype(jnp.float32)
-        weight_buf[0:OWN_BEAMS, cols] = (jnp.where(cos_neg, -cos_mag, cos_mag) * good).astype(
+        weight_buf[0:OWN_BEAMS, cols] = jnp.where(cos_neg, -cos_mag, cos_mag).astype(jnp.bfloat16)
+        weight_buf[OWN_BEAMS : 2 * OWN_BEAMS, cols] = jnp.where(sin_neg, -sin_mag, sin_mag).astype(
             jnp.bfloat16
         )
-        weight_buf[OWN_BEAMS : 2 * OWN_BEAMS, cols] = (
-            jnp.where(sin_neg, -sin_mag, sin_mag) * good
-        ).astype(jnp.bfloat16)
 
     weight_copy = pltpu.make_async_copy(weight_buf, weights, out_sem)
     weight_copy.start()
 
-    for h in range(2):
-        for n in range(SUBS):
-            step_two(h, n)
+    step_two(1, 0)
+    step_two(1, 1)
 
     p_own.wait()
     for copy in p_copies:
@@ -381,54 +374,32 @@
 
 
 def correlate_kernel(
-    spectra, powers, flags, weights, vis, beam,
-    block, power_buf, flag_buf, weight_buf, product, col_scale, row_scale,
-    in_sem, small_sem, out_sem,
+    spectra, powers, flags, flag_row, weights, vis, beam,
+    product, col_scale, row_scale, out_sem,
 ):
     feed = lax.axis_index("feed")
-    power_copy = pltpu.make_async_copy(powers, power_buf, small_sem.at[0])
-    flag_copy = pltpu.make_async_copy(flags, flag_buf, small_sem.at[1])
-    weight_copy = pltpu.make_async_copy(weights, weight_buf, small_sem.at[2])
-
-    def loads(c):
-        rows = pl.ds(pl.multiple_of(c * OWN, OWN), OWN)
-        step = CHAN_DEVS // IN_PARTS
-        return [
-            pltpu.make_async_copy(
-                spectra.at[h, pl.ds(n * step, step), :, rows, :],
-                block.at[c, h, pl.ds(n * step, step)],
-                in_sem.at[c],
-            )
-            for n in range(IN_PARTS)
-            for h in range(2)
-        ]
-
-    power_copy.start()
-    flag_copy.start()
-    for c in range(PER_CHAN):
-        for copy in loads(c):
-            copy.start()
-    weight_copy.start()
-    power_copy.wait()
-    flag_copy.wait()
     lane = lax.broadcasted_iota(jnp.int32, (CHAN_DEVS, 128), 1)
     power = jnp.zeros((CHAN_DEVS, 128), jnp.float32)
     for f in range(FEED_DEVS):
-        power = jnp.where(lane // OWN == f, power_buf[f].reshape(CHAN_DEVS, 128), power)
+        power = jnp.where(lane // OWN == f, powers[f].reshape(CHAN_DEVS, 128), power)
     scale = lax.rsqrt(power / (BAND * NT) + EPSILON)
-    col_scale[...] = scale * flag_buf[...].astype(jnp.float32)
+    col_scale[...] = scale * flags[...].astype(jnp.float32)
     for n in range(2):
         one = col_scale[pl.ds(2 * feed + n, 1), :] * (1.0 / NT)
         row_scale[128 * n : 128 * (n + 1), :] = jnp.broadcast_to(one, (128, 128)).T
 
     def parts(c, first, count):
         return jnp.concatenate(
-            [block[c, h, pl.ds(first, count)].reshape(count * 128, 128) for h in range(2)],
+            [
+                spectra[h, pl.ds(first, count), :, pl.ds(c * OWN, OWN), :].reshape(count * 128, 128)
+                for h in range(2)
+            ],
             axis=1,
         )
 
     def swapped(c, h):
-        own = block[c, h, pl.ds(2 * feed, 2)].reshape(256, 128).astype(jnp.float32)
+        own = spectra[h, pl.ds(2 * feed, 2), :, pl.ds(c * OWN, OWN), :]
+        own = own.reshape(256, 128).astype(jnp.float32)
         lane = lax.broadcasted_iota(jnp.int32, (256, 128), 1)
         turned = pltpu.roll(own, HALF_T, 1)
         return jnp.where(lane < HALF_T, turned, -turned).astype(jnp.bfloat16)
@@ -448,7 +419,6 @@
 
     @pl.loop(0, PER_CHAN)
     def _(c):
-        pltpu.make_async_copy(block.at[c], block.at[c], in_sem.at[c]).wait()
 
         own = parts(c, 2 * feed, 2)
         turned = jnp.concatenate([swapped(c, 0), swapped(c, 1)], axis=1)
@@ -469,11 +439,11 @@
         for copy in stores(c):
             copy.start()
 
-    weight_copy.wait()
+    good = weights[...] * flag_row[...].astype(jnp.float32).astype(jnp.bfloat16)
     lane = lax.broadcasted_iota(jnp.int32, (OWN_BEAMS, 128), 1)
     for c in range(PER_CHAN):
         sums = jnp.dot(
-            weight_buf[...], parts(c, 0, CHAN_DEVS), preferred_element_type=jnp.float32
+            good, parts(c, 0, CHAN_DEVS), preferred_element_type=jnp.float32
         )
         halves = []
         for h in range(2):
@@ -489,7 +459,7 @@
         pltpu.make_async_copy(whole, whole, out_sem.at[c]).wait()
 
 
-def channelize_turn(table, raw_volts, channel_gains, feed_flags, steer_index):
+def channelize_turn(table, raw_volts, channel_gains, steer_index):
     hbm = pl.BlockSpec(memory_space=pl.ANY)
     bf16, f32 = jnp.bfloat16, jnp.float32
     dma = pltpu.SemaphoreType.DMA
@@ -501,7 +471,7 @@
             jax.ShapeDtypeStruct((FEED_DEVS, CHAN_DEVS, 1, 128), f32),
             jax.ShapeDtypeStruct((2 * OWN_BEAMS, INPUTS), bf16),
         ),
-        in_specs=[hbm] * 5,
+        in_specs=[hbm] * 4,
         out_specs=(hbm, hbm, hbm),
         scratch_shapes=[
             pltpu.VMEM((SLABS * OWN, BLOCK), bf16),
@@ -512,7 +482,6 @@
             pltpu.VMEM((2, BAND * OWN, 128), bf16),
             pltpu.VMEM((2, OWN, BAND), f32),
             pltpu.VMEM((BEAMS, FEED_INPUTS), jnp.int32),
-            pltpu.VMEM((1, INPUTS), jnp.int32),
             pltpu.VMEM((8, 8, 128), f32),
             pltpu.VMEM((1, 128), f32),
             pltpu.VMEM((BEAMS, FEED_INPUTS), bf16),
@@ -535,17 +504,17 @@
             dma,
         ],
         compiler_params=pltpu.CompilerParams(
-            collective_id=0, has_side_effects=True, vmem_limit_bytes=60 * 2**20
+            collective_id=0, has_side_effects=True, vmem_limit_bytes=46000 * 1024
         ),
         cost_estimate=pl.CostEstimate(
             flops=2 * SLABS * OWN * BLOCK * 512, bytes_accessed=20_000_000, transcendentals=0
         ),
-    )(raw_volts, table, jnp.transpose(channel_gains, (0, 2, 1)), steer_index, feed_flags.reshape(1, INPUTS))
+    )(raw_volts, table, jnp.transpose(channel_gains, (0, 2, 1)), steer_index)
     return spectra, powers, weights
 
 
 def correlate(spectra, powers, feed_flags, weights):
-    bf16, f32 = jnp.bfloat16, jnp.float32
+    f32 = jnp.float32
     hbm = pl.BlockSpec(memory_space=pl.ANY)
     vmem = pl.BlockSpec(memory_space=pltpu.VMEM)
     dma = pltpu.SemaphoreType.DMA
@@ -556,35 +525,29 @@
             jax.ShapeDtypeStruct((2, PER_CHAN, FEED_INPUTS, INPUTS), f32),
             jax.ShapeDtypeStruct((OWN_BEAMS, PER_CHAN, NT), f32),
         ),
-        in_specs=[hbm] * 4,
+        in_specs=[vmem] * 5,
         out_specs=(hbm, vmem),
         scratch_shapes=[
-            pltpu.VMEM((PER_CHAN, 2, CHAN_DEVS, FEED_DEVS, OWN, 128), bf16),
-            pltpu.VMEM((FEED_DEVS, CHAN_DEVS, 1, 128), f32),
-            pltpu.VMEM((CHAN_DEVS, 128), jnp.int32),
-            pltpu.VMEM((2 * OWN_BEAMS, INPUTS), bf16),
             pltpu.VMEM((2, PER_CHAN, FEED_INPUTS, INPUTS), f32),
             pltpu.VMEM((CHAN_DEVS, 128), f32),
             pltpu.VMEM((256, 128), f32),
             dma((PER_CHAN,)),
-            dma((3,)),
-            dma((PER_CHAN,)),
         ],
-        compiler_params=pltpu.CompilerParams(vmem_limit_bytes=60 * 2**20),
+        compiler_params=pltpu.CompilerParams(vmem_limit_bytes=28 * 2**20),
         cost_estimate=pl.CostEstimate(
             flops=2_700_000_000, bytes_accessed=22_000_000, transcendentals=0
         ),
-    )(spectra, powers, feed_flags.reshape(CHAN_DEVS, 128), weights)
+    )(spectra, powers, feed_flags.reshape(CHAN_DEVS, 128), feed_flags.reshape(1, INPUTS), weights)
 
 
 def solution(mesh):
-    table = filter_table()
+    table = np.stack([filter_table()] * 4)
     in_specs = (P(("chan", "feed"), None), P(None, None, ("chan", "feed")), P(), P(None, "feed"))
     out_specs = (P(None, "chan", "feed", None), P("feed", "chan", None))
 
     def body(raw_volts, channel_gains, feed_flags, steer_index):
         spectra, powers, weights = channelize_turn(
-            jnp.asarray(table), raw_volts, channel_gains, feed_flags, steer_index
+            jnp.asarray(table), raw_volts, channel_gains, steer_index
         )
         return correlate(spectra, powers, feed_flags, weights)
 

time: 59.8 us -> 58.8 us (0.983)
  Pallas kernels: 58.7 us -> 56.2 us
  local copies, waits for them, and re-layouts: 0 us -> 1.76 us
    pallas_call x1, Pallas kernels: 9.15 us -> 7.38 us  [correlate(): pl.pallas_call(correlate_kernel, name='correlate', out_shape=(jax.ShapeDt...]
    unnamed x0 -> x6, local copies, waits for them, and re-layouts: none -> 1.76 us
    pallas_call x1, Pallas kernels: 49.5 us -> 48.8 us  [channelize_turn(): pl.pallas_call(turn_kernel, name='channelize_turn', out_shape=(jax.ShapeD...]
where the time goes in v3:
time: 58.8 us; the launch traced here: 58.6 us
  Pallas kernels  56.2 us (96%)
  local copies, waits for them, and re-layouts  1.76 us (3%)
  between operations  0.66 us (1%)
    pallas_call x1, Pallas kernels, channelize_turn(): pl.pallas_call(turn_kernel, name='channelize_turn', out_shape=(jax.ShapeD...  48.8 us
    pallas_call x1, Pallas kernels, correlate(): pl.pallas_call(correlate_kernel, name='correlate', out_shape=(jax.ShapeDt...  7.38 us
    unnamed x6, local copies, waits for them, and re-layouts  1.76 us

profile of v3, /device:TPU:0, one launch (start us, length us, event | category | flops | bytes accessed | tf_op | source)
XLA Modules:
  0.0 58.6 jit_solution(10709611938117475520)
XLA Ops:
  0.6 0.0 copy-start
  0.6 1.0 %copy-done = s32[512,256]{1,0:T(8,128)S(1)} copy-done((s32[512,256]{1,0:T(8,128)S(1)}, s32[512,256]{1,0:T(8,128)}, u32[]{:S(2)}) %copy-start) | copy-done | bytes 524312
  1.7 0.0 copy-start.1
  1.7 0.7 %copy-done.1 = f32[2,64,16]{1,2,0:T(8,128)S(1)} copy-done((f32[2,64,16]{1,2,0:T(8,128)S(1)}, f32[2,64,16]{1,2,0:T(8,128)}, u32[]{:S(2)}) %copy-start.1) | copy-done | bytes 8216
  2.4 0.0 copy-start.2
  2.4 48.8 %channelize_turn.1 = (bf16[2,16,8,64,128]{4,3,2,1,0:T(8,128)(2,1)S(1)}, f32[8,16,1,128]{3,2,1,0:T(1,128)S(1)}, bf16[128,2048]{1,0:T(8,128)(2,1)S(1)}) custom-call(bf16[16,268288]{1,0:T(8,128)(2,1)} %raw.1, bf16[4,2048,512]{2,1,0:T(8,128)(2,1)} %constant.2.clone.table, f32[2,16,64]{2,1,0:T(8,128)S(1)} %bitcast.3, s32[512,256]{1,0:T(8,128)S(1)} %copy-done), custom_call_target="tpu_custom_call" | custom-call | flops 4395630592 | bytes 20000000 | tf_op jit(solution)/shard_map/channelize_turn/pallas_call | solution.py:466
  51.2 0.0 copy-done.2
  51.2 7.4 %correlate.1 = (f32[2,4,256,2048]{3,2,1,0:T(8,128)}, f32[64,4,128]{2,1,0:T(4,128)}) custom-call(bf16[2,16,8,64,128]{4,3,2,1,0:T(8,128)(2,1)S(1)} %get-tuple-element.5.spectra, f32[8,16,1,128]{3,2,1,0:T(1,128)S(1)} %get-tuple-element.6.powers, s32[16,128]{1,0:T(8,128)S(1)} %bitcast.4, s32[1,2048]{1,0:T(1,128)S(1)} %bitcast.5, ...), custom_call_target="tpu_custom_call" | custom-call | flops 2700000000 | bytes 22000000 | tf_op jit(solution)/shard_map/correlate/pallas_call | solution.py:521
Async XLA Ops:
  0.6 1.0 %copy-start = (s32[512,256]{1,0:T(8,128)S(1)}, s32[512,256]{1,0:T(8,128)}, u32[]{:S(2)}) copy-start(s32[512,256]{1,0:T(8,128)} %steer.1) | copy-start | bytes 1572868
  1.7 0.7 %copy-start.1 = (f32[2,64,16]{1,2,0:T(8,128)S(1)}, f32[2,64,16]{1,2,0:T(8,128)}, u32[]{:S(2)}) copy-start(f32[2,64,16]{1,2,0:T(8,128)} %param.6) | copy-start | bytes 24580
  2.4 48.8 %copy-start.2 = (s32[2048]{0:T(1024)S(1)}, s32[2048]{0:T(1024)}, u32[]{:S(2)}) copy-start(s32[2048]{0:T(1024)} %param.7) | copy-start | bytes 24580

commit v4 on v3

--- a/solution.py
+++ b/solution.py
@@ -26,7 +26,7 @@
 UNIT = PER_CHAN * OWN
 HALF_T = NT // 2
 SLABS = NT + TAPS - 1
-SUBS = 2
+SUBS = 4
 SUB = CHAN_DEVS // SUBS
 OWN_BEAMS = BEAMS // FEED_DEVS
 FEED_INPUTS = INPUTS // FEED_DEVS
@@ -78,9 +78,13 @@
         if (half, d, across) != (0, 0, 0)
     ]
 
+    def near(k):
+        if SUBS == 2:
+            return (chan // SUB + k) % 2
+        return (chan // 8 + k // 2) % 2 * 2 + (chan // 4 + k) % 2
+
     def plane_peer(half, d):
-        first = (chan // SUB + half) % SUBS * SUB
-        return first + lax.rem(chan + d, SUB)
+        return near(half) * SUB + lax.rem(chan + d, SUB)
 
     distant = [(dx, across) for dx in (1, 3, 2) for across in (False, True)]
     for (half, d), across in plane:
@@ -102,7 +106,9 @@
     steer_copy = pltpu.make_async_copy(steer, steer_buf, small_sem.at[1])
     steer_copy.start()
     groups = [(0, 34), (34, 34), (68, 32), (100, 31)]
-    for g, (first, count) in enumerate(groups):
+
+    def fetch(g):
+        first, count = groups[g]
 
         @pl.loop(0, count)
         def _(n):
@@ -112,6 +118,9 @@
                 volts.at[pl.ds(pl.multiple_of(s * OWN, OWN), OWN), :],
                 load_sem.at[g],
             ).start()
+
+    fetch(0)
+    fetch(1)
 
     gain_copy.wait()
     pair_re = jnp.concatenate([gain_buf[0, 0:8], gain_buf[0, 8:16]], axis=1)
@@ -185,7 +194,7 @@
         rows = spectra.at[h, pl.ds(0, count), 0]
         pltpu.make_async_copy(rows, rows, a_recv.at[h, across, half]).wait()
 
-    sub_of = [chan // SUB, 1 - chan // SUB]
+    sub_of = [near(k) for k in range(SUBS)]
 
     def spread(h, n, kind, origin, target):
         block = spectra.at[h, pl.ds(pl.multiple_of(sub_of[n] * SUB, SUB), SUB), origin]
@@ -200,7 +209,7 @@
 
     plans = []
     for n in range(SUBS):
-        fore, back, s = (right, left, 1) if n == 0 else (left, right, -1)
+        fore, back, s = (right, left, 1) if n % 2 == 0 else (left, right, -1)
         plans.append(
             {
                 "own fore": (feed, fore),
@@ -243,6 +252,8 @@
 
     loaded(0)
     tab_copy.wait()
+    fetch(2)
+    fetch(3)
     convolve(0, 34)
 
     steer_copy.wait()
@@ -280,7 +291,12 @@
     step_one(0, 0, mine0)
     turn(1)
     mine1 = send_chan(1)
-    step_one(0, 1, mine0)
+    for n in range(1, SUBS):
+        step_one(0, n, mine0)
+
+    for n in range(SUBS):
+        step_two(0, n)
+        step_one(1, n, mine1)
 
     sums = jnp.sum(power_acc[...], axis=1)
     first = jnp.sum(jnp.where(low8, sums, 0.0), axis=1, keepdims=True)
@@ -306,11 +322,6 @@
         copy.start()
         p_copies.append(copy)
 
-    step_two(0, 0)
-    step_one(1, 0, mine1)
-    step_two(0, 1)
-    step_one(1, 1, mine1)
-
     for copy in steer_copies:
         copy.wait()
     own_steer.wait()
@@ -337,8 +348,8 @@
     weight_copy = pltpu.make_async_copy(weight_buf, weights, out_sem)
     weight_copy.start()
 
-    step_two(1, 0)
-    step_two(1, 1)
+    for n in range(SUBS):
+        step_two(1, n)
 
     p_own.wait()
     for copy in p_copies:

time: 58.8 us -> 58.6 us (level)
  Pallas kernels: 56.2 us -> 55.6 us
    pallas_call x1, Pallas kernels: 48.8 us -> 48.2 us  [channelize_turn(): pl.pallas_call(turn_kernel, name='channelize_turn', out_shape=(jax.ShapeD...]
where the time goes in v4:
time: 58.6 us; the launch traced here: 58 us
  Pallas kernels  55.6 us (95%)
  local copies, waits for them, and re-layouts  1.76 us (3%)
  between operations  0.66 us (1%)
    pallas_call x1, Pallas kernels, channelize_turn(): pl.pallas_call(turn_kernel, name='channelize_turn', out_shape=(jax.ShapeD...  48.2 us
    pallas_call x1, Pallas kernels, correlate(): pl.pallas_call(correlate_kernel, name='correlate', out_shape=(jax.ShapeDt...  7.38 us
    unnamed x6, local copies, waits for them, and re-layouts  1.76 us

profile of v4, /device:TPU:0, one launch (start us, length us, event | category | flops | bytes accessed | tf_op | source)
XLA Modules:
  0.0 58.0 jit_solution(4442814645475078432)
XLA Ops:
  0.6 0.0 copy-start
  0.6 1.0 %copy-done = s32[512,256]{1,0:T(8,128)S(1)} copy-done((s32[512,256]{1,0:T(8,128)S(1)}, s32[512,256]{1,0:T(8,128)}, u32[]{:S(2)}) %copy-start) | copy-done | bytes 524312
  1.7 0.0 copy-start.1
  1.7 0.7 %copy-done.1 = f32[2,64,16]{1,2,0:T(8,128)S(1)} copy-done((f32[2,64,16]{1,2,0:T(8,128)S(1)}, f32[2,64,16]{1,2,0:T(8,128)}, u32[]{:S(2)}) %copy-start.1) | copy-done | bytes 8216
  2.4 0.0 copy-start.2
  2.4 48.2 %channelize_turn.1 = (bf16[2,16,8,64,128]{4,3,2,1,0:T(8,128)(2,1)S(1)}, f32[8,16,1,128]{3,2,1,0:T(1,128)S(1)}, bf16[128,2048]{1,0:T(8,128)(2,1)S(1)}) custom-call(bf16[16,268288]{1,0:T(8,128)(2,1)} %raw.1, bf16[4,2048,512]{2,1,0:T(8,128)(2,1)} %constant.2.clone.table, f32[2,16,64]{2,1,0:T(8,128)S(1)} %bitcast.3, s32[512,256]{1,0:T(8,128)S(1)} %copy-done), custom_call_target="tpu_custom_call" | custom-call | flops 4395630592 | bytes 20000000 | tf_op jit(solution)/shard_map/channelize_turn/pallas_call | solution.py:477
  50.6 0.0 copy-done.2
  50.6 7.4 %correlate.1 = (f32[2,4,256,2048]{3,2,1,0:T(8,128)}, f32[64,4,128]{2,1,0:T(4,128)}) custom-call(bf16[2,16,8,64,128]{4,3,2,1,0:T(8,128)(2,1)S(1)} %get-tuple-element.5.spectra, f32[8,16,1,128]{3,2,1,0:T(1,128)S(1)} %get-tuple-element.6.powers, s32[16,128]{1,0:T(8,128)S(1)} %bitcast.4, s32[1,2048]{1,0:T(1,128)S(1)} %bitcast.5, ...), custom_call_target="tpu_custom_call" | custom-call | flops 2700000000 | bytes 22000000 | tf_op jit(solution)/shard_map/correlate/pallas_call | solution.py:532
Async XLA Ops:
  0.6 1.0 %copy-start = (s32[512,256]{1,0:T(8,128)S(1)}, s32[512,256]{1,0:T(8,128)}, u32[]{:S(2)}) copy-start(s32[512,256]{1,0:T(8,128)} %steer.1) | copy-start | bytes 1572868
  1.7 0.7 %copy-start.1 = (f32[2,64,16]{1,2,0:T(8,128)S(1)}, f32[2,64,16]{1,2,0:T(8,128)}, u32[]{:S(2)}) copy-start(f32[2,64,16]{1,2,0:T(8,128)} %param.6) | copy-start | bytes 24580
  2.4 48.2 %copy-start.2 = (s32[2048]{0:T(1024)S(1)}, s32[2048]{0:T(1024)}, u32[]{:S(2)}) copy-start(s32[2048]{0:T(1024)} %param.7) | copy-start | bytes 24580

commit v5 on v4

--- a/solution.py
+++ b/solution.py
@@ -145,7 +145,7 @@
         for k in range(TAPS):
             part = conv[pl.ds((HALF_T * h + k) * OWN, HALF_T * OWN), 128 * k : 128 * (k + 1)]
             total = part if total is None else total + part
-        summed[...] = total
+        summed[0 : HALF_T * OWN, :] = total
         for i in range(8):
             a = summed[pl.ds(i, HALF_T, stride=OWN), :]
             b = summed[pl.ds(i + 8, HALF_T, stride=OWN), :]
@@ -164,7 +164,7 @@
             flipped = jnp.concatenate([spec_re, spec_im], axis=0).T
             turned[pl.ds(i, BAND, stride=OWN), :] = flipped[0:BAND]
             turned[pl.ds(i + 8, BAND, stride=OWN), :] = flipped[BAND : 2 * BAND]
-        outbox[h] = turned[...].astype(jnp.bfloat16)
+        outbox[h] = turned[0 : BAND * OWN, :].astype(jnp.bfloat16)
 
     a_copies = []
 
@@ -488,8 +488,8 @@
             pltpu.VMEM((SLABS * OWN, BLOCK), bf16),
             pltpu.VMEM((BLOCK, TAPS * 128), bf16),
             pltpu.VMEM((SLABS * OWN, TAPS * 128), f32),
-            pltpu.VMEM((HALF_T * OWN, 128), f32),
-            pltpu.VMEM((BAND * OWN, 128), f32),
+            pltpu.VMEM(((HALF_T + 1) * OWN, 128), f32),
+            pltpu.VMEM(((BAND + 1) * OWN, 128), f32),
             pltpu.VMEM((2, BAND * OWN, 128), bf16),
             pltpu.VMEM((2, OWN, BAND), f32),
             pltpu.VMEM((BEAMS, FEED_INPUTS), jnp.int32),

time: 58.6 us -> 58.6 us (level)
  no operation moved by 1% of the time
where the time goes in v5:
time: 58.6 us; the launch traced here: 58 us
  Pallas kernels  55.6 us (95%)
  local copies, waits for them, and re-layouts  1.76 us (3%)
  between operations  0.66 us (1%)
    pallas_call x1, Pallas kernels, channelize_turn(): pl.pallas_call(turn_kernel, name='channelize_turn', out_shape=(jax.ShapeD...  48.2 us
    pallas_call x1, Pallas kernels, correlate(): pl.pallas_call(correlate_kernel, name='correlate', out_shape=(jax.ShapeDt...  7.38 us
    unnamed x6, local copies, waits for them, and re-layouts  1.76 us

profile of v5, /device:TPU:0, one launch (start us, length us, event | category | flops | bytes accessed | tf_op | source)
XLA Modules:
  0.0 58.0 jit_solution(3313505752981374348)
XLA Ops:
  0.6 0.0 copy-start
  0.6 1.0 %copy-done = s32[512,256]{1,0:T(8,128)S(1)} copy-done((s32[512,256]{1,0:T(8,128)S(1)}, s32[512,256]{1,0:T(8,128)}, u32[]{:S(2)}) %copy-start) | copy-done | bytes 524312
  1.7 0.0 copy-start.1
  1.7 0.7 %copy-done.1 = f32[2,64,16]{1,2,0:T(8,128)S(1)} copy-done((f32[2,64,16]{1,2,0:T(8,128)S(1)}, f32[2,64,16]{1,2,0:T(8,128)}, u32[]{:S(2)}) %copy-start.1) | copy-done | bytes 8216
  2.4 0.0 copy-start.2
  2.4 48.2 %channelize_turn.1 = (bf16[2,16,8,64,128]{4,3,2,1,0:T(8,128)(2,1)S(1)}, f32[8,16,1,128]{3,2,1,0:T(1,128)S(1)}, bf16[128,2048]{1,0:T(8,128)(2,1)S(1)}) custom-call(bf16[16,268288]{1,0:T(8,128)(2,1)} %raw.1, bf16[4,2048,512]{2,1,0:T(8,128)(2,1)} %constant.2.clone.table, f32[2,16,64]{2,1,0:T(8,128)S(1)} %bitcast.3, s32[512,256]{1,0:T(8,128)S(1)} %copy-done), custom_call_target="tpu_custom_call" | custom-call | flops 4395630592 | bytes 20000000 | tf_op jit(solution)/shard_map/channelize_turn/pallas_call | solution.py:477
  50.6 0.0 copy-done.2
  50.6 7.4 %correlate.1 = (f32[2,4,256,2048]{3,2,1,0:T(8,128)}, f32[64,4,128]{2,1,0:T(4,128)}) custom-call(bf16[2,16,8,64,128]{4,3,2,1,0:T(8,128)(2,1)S(1)} %get-tuple-element.5.spectra, f32[8,16,1,128]{3,2,1,0:T(1,128)S(1)} %get-tuple-element.6.powers, s32[16,128]{1,0:T(8,128)S(1)} %bitcast.4, s32[1,2048]{1,0:T(1,128)S(1)} %bitcast.5, ...), custom_call_target="tpu_custom_call" | custom-call | flops 2700000000 | bytes 22000000 | tf_op jit(solution)/shard_map/correlate/pallas_call | solution.py:532
Async XLA Ops:
  0.6 1.0 %copy-start = (s32[512,256]{1,0:T(8,128)S(1)}, s32[512,256]{1,0:T(8,128)}, u32[]{:S(2)}) copy-start(s32[512,256]{1,0:T(8,128)} %steer.1) | copy-start | bytes 1572868
  1.7 0.7 %copy-start.1 = (f32[2,64,16]{1,2,0:T(8,128)S(1)}, f32[2,64,16]{1,2,0:T(8,128)}, u32[]{:S(2)}) copy-start(f32[2,64,16]{1,2,0:T(8,128)} %param.6) | copy-start | bytes 24580
  2.4 48.2 %copy-start.2 = (s32[2048]{0:T(1024)S(1)}, s32[2048]{0:T(1024)}, u32[]{:S(2)}) copy-start(s32[2048]{0:T(1024)} %param.7) | copy-start | bytes 24580
